TPU v7x, 32 devices: a whole 2x2x4 slice. The times are simulated.
32 devices in a mesh: row: 8 (over y, x, core), col: 4 (over z).
Axes of the slice: x: 2, y: 2, z: 4, core: 2. Of those that a mesh axis runs over, the one named last changes fastest.
Arguments:
- image: float32 [1024, 512], P('row', 'col'), may hold values from -10.1 to 10.1
Outputs:
- features: bfloat16 [12, 1024, 512], P(None, 'row', 'col')
All inputs are finite; a program needn't handle non-finite values.
Results may differ from a plain program's by a relative error of at most 0.0014.
Values sent between devices are 32-bit elements; how exact they have to be, the bound alone decides.
No kernel may reach another device: no remote copies, remote signals or barrier semaphores. Data moves between devices by JAX's collectives and lax.ppermute only.
A program may use at most 64 MiB of HBM per device.

v0:
```python
import math

import jax
import jax.numpy as jnp
import numpy as np
from jax import lax
from jax.sharding import PartitionSpec as P

SIG_A = 128
SIG_B = 256


DER_FIRST = (
    1.0 / 280,
    -4.0 / 105,
    1.0 / 5,
    -4.0 / 5,
    0.0,
    4.0 / 5,
    -1.0 / 5,
    4.0 / 105,
    -1.0 / 280,
)
DER_SECOND = (
    -1.0 / 560,
    8.0 / 315,
    -1.0 / 5,
    8.0 / 5,
    -205.0 / 72,
    8.0 / 5,
    -1.0 / 5,
    8.0 / 315,
    -1.0 / 560,
)
DERICHE_POLES = ((1.68, 3.735, 1.783, 0.6318), (-0.6803, -0.2598, 1.723, 1.997))
HIGHEST = lax.Precision.HIGHEST


def passed_along(value, axis, steps):
    count = lax.axis_size(axis)
    leading, last = (max(0, -steps), min(count, count - steps))
    return lax.ppermute(value, axis, [(source, source + steps) for source in range(leading, last)])


def extended(block, sides, width):
    for axis, dim in sides:
        count = lax.axis_size(axis)
        forward = [(i, i + 1) for i in range(count - 1)]
        backward = [(target, source) for source, target in forward]
        low = lax.ppermute(
            lax.slice_in_dim(block, block.shape[dim] - width, None, axis=dim), axis, forward
        )
        high = lax.ppermute(lax.slice_in_dim(block, 0, width, axis=dim), axis, backward)
        block = jnp.concatenate([low, block, high], axis=dim)
    return block


def table(values):
    return jnp.asarray(values, dtype=jnp.float32)


def pole_values(deviation):
    normal_sum = 0.0
    for cos_weight, sin_weight, decay, freq in DERICHE_POLES:
        magnitude = math.exp(-decay / deviation)
        real_z = magnitude * math.cos(freq / deviation)
        imag_z = magnitude * math.sin(freq / deviation)
        denom = (1.0 - real_z) ** 2 + imag_z**2
        real_q = (real_z - magnitude * magnitude) / denom
        imag_q = imag_z / denom
        normal_sum += cos_weight + 2.0 * (cos_weight * real_q + sin_weight * imag_q)
    pole_list = []
    for cos_weight, sin_weight, decay, freq in DERICHE_POLES:
        pole_list.append(
            (cos_weight / normal_sum, -sin_weight / normal_sum, decay / deviation, freq / deviation)
        )
    return pole_list


def pole_power(rate, freq, counts):
    magnitude = np.exp(-rate * counts)
    return (magnitude * np.cos(freq * counts), magnitude * np.sin(freq * counts))


def filter_tables(length, deviation):
    positions = np.arange(length) + 0.0
    distance = np.abs(positions[:, None] - positions[None, :])
    kernel = np.zeros((length, length))
    summary = np.zeros((2, 2, 2, length))
    inject = np.zeros((2, 2, 2, length))
    stride_power = np.zeros((2, 2))
    for index, (real_a, imag_a, rate, freq) in enumerate(pole_values(deviation)):
        dist_re, dist_im = pole_power(rate, freq, distance)
        kernel += real_a * dist_re - imag_a * dist_im
        back_re, back_im = pole_power(rate, freq, length - 1 - positions)
        summary[0, 0, index] = back_re
        summary[0, 1, index] = back_im
        fwd_re, fwd_im = pole_power(rate, freq, positions)
        summary[1, 0, index] = fwd_re
        summary[1, 1, index] = fwd_im
        next_re, next_im = pole_power(rate, freq, positions + 1)
        inject[0, 0, index] = real_a * next_re - imag_a * next_im
        inject[0, 1, index] = -(real_a * next_im + imag_a * next_re)
        rest_re, rest_im = pole_power(rate, freq, length - positions)
        inject[1, 0, index] = real_a * rest_re - imag_a * rest_im
        inject[1, 1, index] = -(real_a * rest_im + imag_a * rest_re)
        whole_re, whole_im = pole_power(rate, freq, length + 0.0)
        stride_power[0, index] = whole_re
        stride_power[1, index] = whole_im
    return (kernel, summary, inject, stride_power)


def tap_sum(source, coeffs, axis, length):
    accum = coeffs[0] * lax.slice_in_dim(source, 0, length, axis=axis)
    for offset in range(1, 9):
        accum = accum + coeffs[offset] * lax.slice_in_dim(
            source, offset, offset + length, axis=axis
        )
    return accum


def derivative_fields(padded, rows, cols):
    along_cols = tap_sum(padded, DER_FIRST, 1, cols)
    center = padded[4 : 4 + rows, 4 : 4 + cols]
    grad_x = along_cols[4 : 4 + rows]
    grad_y = tap_sum(padded[:, 4 : 4 + cols], DER_FIRST, 0, rows)
    curve_xx = tap_sum(padded[4 : 4 + rows], DER_SECOND, 1, cols)
    curve_xy = tap_sum(along_cols, DER_FIRST, 0, rows)
    curve_yy = tap_sum(padded[:, 4 : 4 + cols], DER_SECOND, 0, rows)
    return jnp.stack([center, grad_x, grad_y, curve_xx, curve_xy, curve_yy])


def complex_mul(left, right):
    real_part = left[0] * right[0] - left[1] * right[1]
    imag_part = left[0] * right[1] + left[1] * right[0]
    return jnp.stack([real_part, imag_part])


def chain_carry(local_sum, stride_power, count, mover):

    def advance(index, state):
        return mover(complex_mul(stride_power, state) + local_sum)

    return lax.fori_loop(0, count - 1, advance, jnp.zeros_like(local_sum))


def col_carries(forward, backward, stride_power):
    count = lax.axis_size("col")
    left_in = chain_carry(
        forward, stride_power, count, lambda payload: passed_along(payload, "col", 1)
    )
    right_in = chain_carry(
        backward, stride_power, count, lambda payload: passed_along(payload, "col", -1)
    )
    return (left_in, right_in)


def row_carries(forward, backward, stride_power):
    count = lax.axis_size("row")
    upper_in = chain_carry(
        forward, stride_power, count, lambda payload: passed_along(payload, "row", 1)
    )
    lower_in = chain_carry(
        backward, stride_power, count, lambda payload: passed_along(payload, "row", -1)
    )
    return (upper_in, lower_in)


def on_device(image):
    rows_dev, cols_dev = image.shape
    padded = extended(image, (("row", 0), ("col", 1)), 4)
    fields = derivative_fields(padded, rows_dev, cols_dev)
    deviations = (SIG_A, SIG_B)
    col_tables = [filter_tables(cols_dev, deviation) for deviation in deviations]
    row_tables = [filter_tables(rows_dev, deviation) for deviation in deviations]
    flat_rows = fields.reshape(6 * rows_dev, cols_dev)
    col_summary = np.concatenate([tables[1][:, :, None] for tables in col_tables], axis=2).reshape(
        16, cols_dev
    )
    col_power = np.concatenate([tables[3] for tables in col_tables], axis=1)[:, :, None]
    col_sums = jnp.einsum("kc,fc->kf", table(col_summary), flat_rows, precision=HIGHEST).reshape(
        2, 2, 4, 6 * rows_dev
    )
    left_in, right_in = col_carries(col_sums[0], col_sums[1], table(col_power))
    smoothed = []
    for level in range(2):
        kernel, summary, inject, stride_power = col_tables[level]
        blended = jnp.dot(flat_rows, table(kernel), precision=HIGHEST)
        blended = blended + jnp.einsum(
            "rpf,rpj->fj",
            left_in[:, 2 * level : 2 * level + 2],
            table(inject[0]),
            precision=HIGHEST,
        )
        blended = blended + jnp.einsum(
            "rpf,rpj->fj",
            right_in[:, 2 * level : 2 * level + 2],
            table(inject[1]),
            precision=HIGHEST,
        )
        smoothed.append(blended.reshape(6, rows_dev, cols_dev))
    row_sums = []
    for level in range(2):
        summary = row_tables[level][1].reshape(8, rows_dev)
        partial_sums = jnp.einsum("kj,fjc->kfc", table(summary), smoothed[level], precision=HIGHEST)
        row_sums.append(partial_sums.reshape(2, 2, 2, 6 * cols_dev))
    row_sums = jnp.concatenate(row_sums, axis=2)
    row_power = np.concatenate([tables[3] for tables in row_tables], axis=1)[:, :, None]
    upper_in, lower_in = row_carries(row_sums[0], row_sums[1], table(row_power))
    results = []
    for level in range(2):
        kernel, summary, inject, stride_power = row_tables[level]
        deviation = deviations[level]
        blended = jnp.einsum("ij,fjc->fic", table(kernel), smoothed[level], precision=HIGHEST)
        upper_part = upper_in[:, 2 * level : 2 * level + 2].reshape(2, 2, 6, cols_dev)
        lower_part = lower_in[:, 2 * level : 2 * level + 2].reshape(2, 2, 6, cols_dev)
        blended = blended + jnp.einsum(
            "rpfc,rpi->fic", upper_part, table(inject[0]), precision=HIGHEST
        )
        blended = blended + jnp.einsum(
            "rpfc,rpi->fic", lower_part, table(inject[1]), precision=HIGHEST
        )
        base = 2.0 * math.sqrt(math.pi) * deviation
        factors = jnp.array(
            [
                base,
                base * deviation,
                base * deviation,
                base * deviation**2,
                base * deviation**2,
                base * deviation**2,
            ],
            jnp.float32,
        )
        results.append(blended * factors[:, None, None])
    return jnp.concatenate(results, axis=0).astype(jnp.bfloat16)


def solution(mesh):
    placed = (P("row", "col"),)
    return jax.shard_map(
        on_device, mesh=mesh, in_specs=placed, out_specs=P(None, "row", "col"), check_vma=False
    )
```

profile of v0, /device:TPU:11, one launch (start us, length us, event | category | flops | bytes accessed | tf_op | source)
XLA Modules:
  0.0 155.9 jit_solution(11656665037139778006)
XLA Ops:
  0.7 3.7 %collective-permute-start.4 = (f32[4,128]{1,0:T(4,128)S(1)}, f32[4,128]{1,0:T(4,128)S(1)}, u32[]{:S(2)}, u32[]{:S(2)}) collective-permute-start(f32[4,128]{1,0:T(4,128)S(1)} %get-tuple-element.181), channel_id=1, source_target_pairs={{0,4},{4,8},{8,12},{12,16},{16,20},{20,24},{24,28},{1,5},{5,9},{9,... | collective-permute-start | bytes 6152 | tf_op jit(solution)/shard_map/ppermute | solution.py:50
  4.4 2.1 %collective-permute-start.5 = (f32[4,128]{1,0:T(4,128)S(1)}, f32[4,128]{1,0:T(4,128)S(1)}, u32[]{:S(2)}, u32[]{:S(2)}) collective-permute-start(f32[4,128]{1,0:T(4,128)S(1)} %get-tuple-element.182), channel_id=1, source_target_pairs={{4,0},{8,4},{12,8},{16,12},{20,16},{24,20},{28,24},{5,1},{9,5},{13... | collective-permute-start | bytes 6152 | tf_op jit(solution)/shard_map/ppermute | solution.py:53
  7.3 3.0 %collective-permute-done.5 = f32[4,128]{1,0:T(4,128)S(1)} collective-permute-done((f32[4,128]{1,0:T(4,128)S(1)}, f32[4,128]{1,0:T(4,128)S(1)}, u32[]{:S(2)}, u32[]{:S(2)}) %collective-permute-start.5) | collective-permute-done | bytes 2080 | tf_op jit(solution)/shard_map/ppermute | solution.py:53
  10.4 3.2 %collective-permute-start.6 = (f32[136,4]{1,0:T(8,128)S(1)}, f32[136,4]{1,0:T(8,128)S(1)}, u32[]{:S(2)}, u32[]{:S(2)}) collective-permute-start(f32[136,4]{1,0:T(8,128)S(1)} %get-tuple-element.179), channel_id=1, source_target_pairs={{0,1},{1,2},{2,3},{4,5},{5,6},{6,7},{8,9},{9,10},{10,11},{12,13},{... | collective-permute-start | bytes 6536 | tf_op jit(solution)/shard_map/ppermute | solution.py:50
  13.6 2.1 %collective-permute-start.7 = (f32[136,4]{1,0:T(8,128)S(1)}, f32[136,4]{1,0:T(8,128)S(1)}, u32[]{:S(2)}, u32[]{:S(2)}) collective-permute-start(f32[136,4]{1,0:T(8,128)S(1)} %get-tuple-element.180), channel_id=1, source_target_pairs={{1,0},{2,1},{3,2},{5,4},{6,5},{7,6},{9,8},{10,9},{11,10},{13,12},{... | collective-permute-start | bytes 6536 | tf_op jit(solution)/shard_map/ppermute | solution.py:53
  15.7 2.9 %collective-permute-done.7 = f32[136,4]{1,0:T(8,128)S(1)} collective-permute-done((f32[136,4]{1,0:T(8,128)S(1)}, f32[136,4]{1,0:T(8,128)S(1)}, u32[]{:S(2)}, u32[]{:S(2)}) %collective-permute-start.7) | collective-permute-done | bytes 2208 | tf_op jit(solution)/shard_map/ppermute | solution.py:53
  21.2 14.4 %while.44 = (s32[]{:T(128)}, f32[2,4,768]{2,1,0:T(4,128)S(1)}, f32[2,4,768]{2,1,0:T(4,128)S(1)}, s32[]{:T(128)}, f32[4]{0:T(128)S(1)}, /*index=5*/f32[4]{0:T(128)S(1)}) while((s32[]{:T(128)}, f32[2,4,768]{2,1,0:T(4,128)S(1)}, f32[2,4,768]{2,1,0:T(4,128)S(1)}, s32[]{:T(128)}, f32[4]{0:T(128)S(1)}, ...), condition=%wide.region_1.0_spmd.clone, body=%wide.region_0.0_spmd.sunk.clone.sunk | while | flops 30722 | bytes 221325 | solution.py:144
  21.3 3.2 %collective-permute-start = (f32[2,4,768]{2,1,0:T(4,128)S(1)}, f32[2,4,768]{2,1,0:T(4,128)S(1)}, u32[]{:S(2)}, u32[]{:S(2)}) collective-permute-start(f32[2,4,768]{2,1,0:T(4,128)S(1)} %maximum_add_fusion.8), channel_id=1, source_target_pairs={{0,1},{1,2},{2,3},{4,5},{5,6},{6,7},{8,9},{9,10},{10,11},{12,13},{... | collective-permute-start | bytes 73736 | tf_op jit(solution)/shard_map/while/body/eval_jaxpr/ppermute | solution.py:42
  24.5 1.8 %collective-permute-done = f32[2,4,768]{2,1,0:T(4,128)S(1)} collective-permute-done((f32[2,4,768]{2,1,0:T(4,128)S(1)}, f32[2,4,768]{2,1,0:T(4,128)S(1)}, u32[]{:S(2)}, u32[]{:S(2)}) %collective-permute-start) | collective-permute-done | bytes 24608 | tf_op jit(solution)/shard_map/while/body/eval_jaxpr/ppermute | solution.py:42
  26.4 3.2 %collective-permute-start = (f32[2,4,768]{2,1,0:T(4,128)S(1)}, f32[2,4,768]{2,1,0:T(4,128)S(1)}, u32[]{:S(2)}, u32[]{:S(2)}) collective-permute-start(f32[2,4,768]{2,1,0:T(4,128)S(1)} %maximum_add_fusion.8), channel_id=1, source_target_pairs={{0,1},{1,2},{2,3},{4,5},{5,6},{6,7},{8,9},{9,10},{10,11},{12,13},{... | collective-permute-start | bytes 73736 | tf_op jit(solution)/shard_map/while/body/eval_jaxpr/ppermute | solution.py:42
  29.6 1.4 collective-permute-done
  31.1 3.2 %collective-permute-start = (f32[2,4,768]{2,1,0:T(4,128)S(1)}, f32[2,4,768]{2,1,0:T(4,128)S(1)}, u32[]{:S(2)}, u32[]{:S(2)}) collective-permute-start(f32[2,4,768]{2,1,0:T(4,128)S(1)} %maximum_add_fusion.8), channel_id=1, source_target_pairs={{0,1},{1,2},{2,3},{4,5},{5,6},{6,7},{8,9},{9,10},{10,11},{12,13},{... | collective-permute-start | bytes 73736 | tf_op jit(solution)/shard_map/while/body/eval_jaxpr/ppermute | solution.py:42
  34.3 1.4 collective-permute-done
  37.1 14.0 %while.45 = (s32[]{:T(128)}, f32[2,4,768]{2,1,0:T(4,128)S(1)}, f32[2,4,768]{2,1,0:T(4,128)S(1)}, s32[]{:T(128)}, f32[4]{0:T(128)S(1)}, /*index=5*/f32[4]{0:T(128)S(1)}) while((s32[]{:T(128)}, f32[2,4,768]{2,1,0:T(4,128)S(1)}, f32[2,4,768]{2,1,0:T(4,128)S(1)}, s32[]{:T(128)}, f32[4]{0:T(128)S(1)}, ...), condition=%wide.region_3.0_spmd.clone, body=%wide.region_2.0_spmd.sunk.clone.sunk | while | flops 30722 | bytes 221325 | solution.py:144
  37.2 1.9 %collective-permute-start.1 = (f32[2,4,768]{2,1,0:T(4,128)S(1)}, f32[2,4,768]{2,1,0:T(4,128)S(1)}, u32[]{:S(2)}, u32[]{:S(2)}) collective-permute-start(f32[2,4,768]{2,1,0:T(4,128)S(1)} %maximum_add_fusion.9), channel_id=1, source_target_pairs={{1,0},{2,1},{3,2},{5,4},{6,5},{7,6},{9,8},{10,9},{11,10},{13,12},{... | collective-permute-start | bytes 73736 | tf_op jit(solution)/shard_map/while/body/eval_jaxpr/ppermute | solution.py:42
  39.2 2.6 %collective-permute-done.1 = f32[2,4,768]{2,1,0:T(4,128)S(1)} collective-permute-done((f32[2,4,768]{2,1,0:T(4,128)S(1)}, f32[2,4,768]{2,1,0:T(4,128)S(1)}, u32[]{:S(2)}, u32[]{:S(2)}) %collective-permute-start.1) | collective-permute-done | bytes 24608 | tf_op jit(solution)/shard_map/while/body/eval_jaxpr/ppermute | solution.py:42
  41.9 1.9 %collective-permute-start.1 = (f32[2,4,768]{2,1,0:T(4,128)S(1)}, f32[2,4,768]{2,1,0:T(4,128)S(1)}, u32[]{:S(2)}, u32[]{:S(2)}) collective-permute-start(f32[2,4,768]{2,1,0:T(4,128)S(1)} %maximum_add_fusion.9), channel_id=1, source_target_pairs={{1,0},{2,1},{3,2},{5,4},{6,5},{7,6},{9,8},{10,9},{11,10},{13,12},{... | collective-permute-start | bytes 73736 | tf_op jit(solution)/shard_map/while/body/eval_jaxpr/ppermute | solution.py:42
  43.8 2.6 %collective-permute-done.1 = f32[2,4,768]{2,1,0:T(4,128)S(1)} collective-permute-done((f32[2,4,768]{2,1,0:T(4,128)S(1)}, f32[2,4,768]{2,1,0:T(4,128)S(1)}, u32[]{:S(2)}, u32[]{:S(2)}) %collective-permute-start.1) | collective-permute-done | bytes 24608 | tf_op jit(solution)/shard_map/while/body/eval_jaxpr/ppermute | solution.py:42
  46.6 1.9 %collective-permute-start.1 = (f32[2,4,768]{2,1,0:T(4,128)S(1)}, f32[2,4,768]{2,1,0:T(4,128)S(1)}, u32[]{:S(2)}, u32[]{:S(2)}) collective-permute-start(f32[2,4,768]{2,1,0:T(4,128)S(1)} %maximum_add_fusion.9), channel_id=1, source_target_pairs={{1,0},{2,1},{3,2},{5,4},{6,5},{7,6},{9,8},{10,9},{11,10},{13,12},{... | collective-permute-start | bytes 73736 | tf_op jit(solution)/shard_map/while/body/eval_jaxpr/ppermute | solution.py:42
  48.5 2.6 %collective-permute-done.1 = f32[2,4,768]{2,1,0:T(4,128)S(1)} collective-permute-done((f32[2,4,768]{2,1,0:T(4,128)S(1)}, f32[2,4,768]{2,1,0:T(4,128)S(1)}, u32[]{:S(2)}, u32[]{:S(2)}) %collective-permute-start.1) | collective-permute-done | bytes 24608 | tf_op jit(solution)/shard_map/while/body/eval_jaxpr/ppermute | solution.py:42
  57.1 47.9 %while.46 = (s32[]{:T(128)}, f32[2,4,768]{2,1,0:T(4,128)S(1)}, f32[2,4,768]{2,1,0:T(4,128)S(1)}, s32[]{:T(128)}, f32[4]{0:T(128)S(1)}, /*index=5*/f32[4]{0:T(128)S(1)}) while((s32[]{:T(128)}, f32[2,4,768]{2,1,0:T(4,128)S(1)}, f32[2,4,768]{2,1,0:T(4,128)S(1)}, s32[]{:T(128)}, f32[4]{0:T(128)S(1)}, ...), condition=%wide.region_5.0_spmd.clone, body=%wide.region_4.0_spmd.sunk.clone.sunk | while | flops 30722 | bytes 221325 | solution.py:144
  57.2 10.1 %collective-permute-start.2 = (f32[2,4,768]{2,1,0:T(4,128)S(1)}, f32[2,4,768]{2,1,0:T(4,128)S(1)}, u32[]{:S(2)}, u32[]{:S(2)}) collective-permute-start(f32[2,4,768]{2,1,0:T(4,128)S(1)} %maximum_add_fusion.10), channel_id=1, source_target_pairs={{0,4},{4,8},{8,12},{12,16},{16,20},{20,24},{24,28},{1,5},{5,9},{9,... | collective-permute-start | bytes 73736 | tf_op jit(solution)/shard_map/while/body/eval_jaxpr/ppermute | solution.py:42
  67.2 0.9 collective-permute-done.2
  68.3 5.1 %collective-permute-start.2 = (f32[2,4,768]{2,1,0:T(4,128)S(1)}, f32[2,4,768]{2,1,0:T(4,128)S(1)}, u32[]{:S(2)}, u32[]{:S(2)}) collective-permute-start(f32[2,4,768]{2,1,0:T(4,128)S(1)} %maximum_add_fusion.10), channel_id=1, source_target_pairs={{0,4},{4,8},{8,12},{12,16},{16,20},{20,24},{24,28},{1,5},{5,9},{9,... | collective-permute-start | bytes 73736 | tf_op jit(solution)/shard_map/while/body/eval_jaxpr/ppermute | solution.py:42
  73.4 0.9 collective-permute-done.2
  74.4 5.1 %collective-permute-start.2 = (f32[2,4,768]{2,1,0:T(4,128)S(1)}, f32[2,4,768]{2,1,0:T(4,128)S(1)}, u32[]{:S(2)}, u32[]{:S(2)}) collective-permute-start(f32[2,4,768]{2,1,0:T(4,128)S(1)} %maximum_add_fusion.10), channel_id=1, source_target_pairs={{0,4},{4,8},{8,12},{12,16},{16,20},{20,24},{24,28},{1,5},{5,9},{9,... | collective-permute-start | bytes 73736 | tf_op jit(solution)/shard_map/while/body/eval_jaxpr/ppermute | solution.py:42
  80.5 5.1 %collective-permute-start.2 = (f32[2,4,768]{2,1,0:T(4,128)S(1)}, f32[2,4,768]{2,1,0:T(4,128)S(1)}, u32[]{:S(2)}, u32[]{:S(2)}) collective-permute-start(f32[2,4,768]{2,1,0:T(4,128)S(1)} %maximum_add_fusion.10), channel_id=1, source_target_pairs={{0,4},{4,8},{8,12},{12,16},{16,20},{20,24},{24,28},{1,5},{5,9},{9,... | collective-permute-start | bytes 73736 | tf_op jit(solution)/shard_map/while/body/eval_jaxpr/ppermute | solution.py:42
  86.7 5.1 %collective-permute-start.2 = (f32[2,4,768]{2,1,0:T(4,128)S(1)}, f32[2,4,768]{2,1,0:T(4,128)S(1)}, u32[]{:S(2)}, u32[]{:S(2)}) collective-permute-start(f32[2,4,768]{2,1,0:T(4,128)S(1)} %maximum_add_fusion.10), channel_id=1, source_target_pairs={{0,4},{4,8},{8,12},{12,16},{16,20},{20,24},{24,28},{1,5},{5,9},{9,... | collective-permute-start | bytes 73736 | tf_op jit(solution)/shard_map/while/body/eval_jaxpr/ppermute | solution.py:42
  91.8 0.9 collective-permute-done.2
  92.8 5.1 %collective-permute-start.2 = (f32[2,4,768]{2,1,0:T(4,128)S(1)}, f32[2,4,768]{2,1,0:T(4,128)S(1)}, u32[]{:S(2)}, u32[]{:S(2)}) collective-permute-start(f32[2,4,768]{2,1,0:T(4,128)S(1)} %maximum_add_fusion.10), channel_id=1, source_target_pairs={{0,4},{4,8},{8,12},{12,16},{16,20},{20,24},{24,28},{1,5},{5,9},{9,... | collective-permute-start | bytes 73736 | tf_op jit(solution)/shard_map/while/body/eval_jaxpr/ppermute | solution.py:42
  97.9 0.9 collective-permute-done.2
  98.9 5.1 %collective-permute-start.2 = (f32[2,4,768]{2,1,0:T(4,128)S(1)}, f32[2,4,768]{2,1,0:T(4,128)S(1)}, u32[]{:S(2)}, u32[]{:S(2)}) collective-permute-start(f32[2,4,768]{2,1,0:T(4,128)S(1)} %maximum_add_fusion.10), channel_id=1, source_target_pairs={{0,4},{4,8},{8,12},{12,16},{16,20},{20,24},{24,28},{1,5},{5,9},{9,... | collective-permute-start | bytes 73736 | tf_op jit(solution)/shard_map/while/body/eval_jaxpr/ppermute | solution.py:42
  105.7 43.5 %while.47 = (s32[]{:T(128)}, f32[2,4,768]{2,1,0:T(4,128)S(1)}, f32[2,4,768]{2,1,0:T(4,128)S(1)}, s32[]{:T(128)}, f32[4]{0:T(128)S(1)}, /*index=5*/f32[4]{0:T(128)S(1)}) while((s32[]{:T(128)}, f32[2,4,768]{2,1,0:T(4,128)S(1)}, f32[2,4,768]{2,1,0:T(4,128)S(1)}, s32[]{:T(128)}, f32[4]{0:T(128)S(1)}, ...), condition=%wide.region_7.0_spmd.clone, body=%wide.region_6.0_spmd.sunk.clone.sunk | while | flops 30722 | bytes 221325 | solution.py:144
  105.8 1.9 %collective-permute-start.3 = (f32[2,4,768]{2,1,0:T(4,128)S(1)}, f32[2,4,768]{2,1,0:T(4,128)S(1)}, u32[]{:S(2)}, u32[]{:S(2)}) collective-permute-start(f32[2,4,768]{2,1,0:T(4,128)S(1)} %maximum_add_fusion.11), channel_id=1, source_target_pairs={{4,0},{8,4},{12,8},{16,12},{20,16},{24,20},{28,24},{5,1},{9,5},{13... | collective-permute-start | bytes 73736 | tf_op jit(solution)/shard_map/while/body/eval_jaxpr/ppermute | solution.py:42
  107.7 4.7 %collective-permute-done.3 = f32[2,4,768]{2,1,0:T(4,128)S(1)} collective-permute-done((f32[2,4,768]{2,1,0:T(4,128)S(1)}, f32[2,4,768]{2,1,0:T(4,128)S(1)}, u32[]{:S(2)}, u32[]{:S(2)}) %collective-permute-start.3) | collective-permute-done | bytes 24608 | tf_op jit(solution)/shard_map/while/body/eval_jaxpr/ppermute | solution.py:42
  112.5 1.9 %collective-permute-start.3 = (f32[2,4,768]{2,1,0:T(4,128)S(1)}, f32[2,4,768]{2,1,0:T(4,128)S(1)}, u32[]{:S(2)}, u32[]{:S(2)}) collective-permute-start(f32[2,4,768]{2,1,0:T(4,128)S(1)} %maximum_add_fusion.11), channel_id=1, source_target_pairs={{4,0},{8,4},{12,8},{16,12},{20,16},{24,20},{28,24},{5,1},{9,5},{13... | collective-permute-start | bytes 73736 | tf_op jit(solution)/shard_map/while/body/eval_jaxpr/ppermute | solution.py:42
  114.4 4.1 %collective-permute-done.3 = f32[2,4,768]{2,1,0:T(4,128)S(1)} collective-permute-done((f32[2,4,768]{2,1,0:T(4,128)S(1)}, f32[2,4,768]{2,1,0:T(4,128)S(1)}, u32[]{:S(2)}, u32[]{:S(2)}) %collective-permute-start.3) | collective-permute-done | bytes 24608 | tf_op jit(solution)/shard_map/while/body/eval_jaxpr/ppermute | solution.py:42
  118.6 1.9 %collective-permute-start.3 = (f32[2,4,768]{2,1,0:T(4,128)S(1)}, f32[2,4,768]{2,1,0:T(4,128)S(1)}, u32[]{:S(2)}, u32[]{:S(2)}) collective-permute-start(f32[2,4,768]{2,1,0:T(4,128)S(1)} %maximum_add_fusion.11), channel_id=1, source_target_pairs={{4,0},{8,4},{12,8},{16,12},{20,16},{24,20},{28,24},{5,1},{9,5},{13... | collective-permute-start | bytes 73736 | tf_op jit(solution)/shard_map/while/body/eval_jaxpr/ppermute | solution.py:42
  120.5 4.1 %collective-permute-done.3 = f32[2,4,768]{2,1,0:T(4,128)S(1)} collective-permute-done((f32[2,4,768]{2,1,0:T(4,128)S(1)}, f32[2,4,768]{2,1,0:T(4,128)S(1)}, u32[]{:S(2)}, u32[]{:S(2)}) %collective-permute-start.3) | collective-permute-done | bytes 24608 | tf_op jit(solution)/shard_map/while/body/eval_jaxpr/ppermute | solution.py:42
  124.7 1.9 %collective-permute-start.3 = (f32[2,4,768]{2,1,0:T(4,128)S(1)}, f32[2,4,768]{2,1,0:T(4,128)S(1)}, u32[]{:S(2)}, u32[]{:S(2)}) collective-permute-start(f32[2,4,768]{2,1,0:T(4,128)S(1)} %maximum_add_fusion.11), channel_id=1, source_target_pairs={{4,0},{8,4},{12,8},{16,12},{20,16},{24,20},{28,24},{5,1},{9,5},{13... | collective-permute-start | bytes 73736 | tf_op jit(solution)/shard_map/while/body/eval_jaxpr/ppermute | solution.py:42
  126.7 4.1 %collective-permute-done.3 = f32[2,4,768]{2,1,0:T(4,128)S(1)} collective-permute-done((f32[2,4,768]{2,1,0:T(4,128)S(1)}, f32[2,4,768]{2,1,0:T(4,128)S(1)}, u32[]{:S(2)}, u32[]{:S(2)}) %collective-permute-start.3) | collective-permute-done | bytes 24608 | tf_op jit(solution)/shard_map/while/body/eval_jaxpr/ppermute | solution.py:42
  130.9 1.9 %collective-permute-start.3 = (f32[2,4,768]{2,1,0:T(4,128)S(1)}, f32[2,4,768]{2,1,0:T(4,128)S(1)}, u32[]{:S(2)}, u32[]{:S(2)}) collective-permute-start(f32[2,4,768]{2,1,0:T(4,128)S(1)} %maximum_add_fusion.11), channel_id=1, source_target_pairs={{4,0},{8,4},{12,8},{16,12},{20,16},{24,20},{28,24},{5,1},{9,5},{13... | collective-permute-start | bytes 73736 | tf_op jit(solution)/shard_map/while/body/eval_jaxpr/ppermute | solution.py:42
  132.8 4.1 %collective-permute-done.3 = f32[2,4,768]{2,1,0:T(4,128)S(1)} collective-permute-done((f32[2,4,768]{2,1,0:T(4,128)S(1)}, f32[2,4,768]{2,1,0:T(4,128)S(1)}, u32[]{:S(2)}, u32[]{:S(2)}) %collective-permute-start.3) | collective-permute-done | bytes 24608 | tf_op jit(solution)/shard_map/while/body/eval_jaxpr/ppermute | solution.py:42
  137.0 1.9 %collective-permute-start.3 = (f32[2,4,768]{2,1,0:T(4,128)S(1)}, f32[2,4,768]{2,1,0:T(4,128)S(1)}, u32[]{:S(2)}, u32[]{:S(2)}) collective-permute-start(f32[2,4,768]{2,1,0:T(4,128)S(1)} %maximum_add_fusion.11), channel_id=1, source_target_pairs={{4,0},{8,4},{12,8},{16,12},{20,16},{24,20},{28,24},{5,1},{9,5},{13... | collective-permute-start | bytes 73736 | tf_op jit(solution)/shard_map/while/body/eval_jaxpr/ppermute | solution.py:42
  138.9 4.1 %collective-permute-done.3 = f32[2,4,768]{2,1,0:T(4,128)S(1)} collective-permute-done((f32[2,4,768]{2,1,0:T(4,128)S(1)}, f32[2,4,768]{2,1,0:T(4,128)S(1)}, u32[]{:S(2)}, u32[]{:S(2)}) %collective-permute-start.3) | collective-permute-done | bytes 24608 | tf_op jit(solution)/shard_map/while/body/eval_jaxpr/ppermute | solution.py:42
  143.2 1.9 %collective-permute-start.3 = (f32[2,4,768]{2,1,0:T(4,128)S(1)}, f32[2,4,768]{2,1,0:T(4,128)S(1)}, u32[]{:S(2)}, u32[]{:S(2)}) collective-permute-start(f32[2,4,768]{2,1,0:T(4,128)S(1)} %maximum_add_fusion.11), channel_id=1, source_target_pairs={{4,0},{8,4},{12,8},{16,12},{20,16},{24,20},{28,24},{5,1},{9,5},{13... | collective-permute-start | bytes 73736 | tf_op jit(solution)/shard_map/while/body/eval_jaxpr/ppermute | solution.py:42
  145.1 4.1 %collective-permute-done.3 = f32[2,4,768]{2,1,0:T(4,128)S(1)} collective-permute-done((f32[2,4,768]{2,1,0:T(4,128)S(1)}, f32[2,4,768]{2,1,0:T(4,128)S(1)}, u32[]{:S(2)}, u32[]{:S(2)}) %collective-permute-start.3) | collective-permute-done | bytes 24608 | tf_op jit(solution)/shard_map/while/body/eval_jaxpr/ppermute | solution.py:42
  155.0 0.9 copy.40
  (144 shorter events, 22.2 us)
Async XLA Ops:
  0.7 6.6 %collective-permute-start.4 = (f32[4,128]{1,0:T(4,128)S(1)}, f32[4,128]{1,0:T(4,128)S(1)}, u32[]{:S(2)}, u32[]{:S(2)}) collective-permute-start(f32[4,128]{1,0:T(4,128)S(1)} %get-tuple-element.181), channel_id=1, source_target_pairs={{0,4},{4,8},{8,12},{12,16},{16,20},{20,24},{24,28},{1,5},{5,9},{9,... | collective-permute-start | bytes 6152 | tf_op jit(solution)/shard_map/ppermute | solution.py:50
  4.4 2.9 %copy-start = (f32[128,128]{1,0:T(8,128)S(1)}, f32[128,128]{1,0:T(8,128)}, u32[]{:S(2)}) copy-start(f32[128,128]{1,0:T(8,128)} %param.28) | copy-start | bytes 196612
  4.4 5.9 %collective-permute-start.5 = (f32[4,128]{1,0:T(4,128)S(1)}, f32[4,128]{1,0:T(4,128)S(1)}, u32[]{:S(2)}, u32[]{:S(2)}) collective-permute-start(f32[4,128]{1,0:T(4,128)S(1)} %get-tuple-element.182), channel_id=1, source_target_pairs={{4,0},{8,4},{12,8},{16,12},{20,16},{24,20},{28,24},{5,1},{9,5},{13... | collective-permute-start | bytes 6152 | tf_op jit(solution)/shard_map/ppermute | solution.py:53
  10.4 5.3 %collective-permute-start.6 = (f32[136,4]{1,0:T(8,128)S(1)}, f32[136,4]{1,0:T(8,128)S(1)}, u32[]{:S(2)}, u32[]{:S(2)}) collective-permute-start(f32[136,4]{1,0:T(8,128)S(1)} %get-tuple-element.179), channel_id=1, source_target_pairs={{0,1},{1,2},{2,3},{4,5},{5,6},{6,7},{8,9},{9,10},{10,11},{12,13},{... | collective-permute-start | bytes 6536 | tf_op jit(solution)/shard_map/ppermute | solution.py:50
  13.6 5.1 %collective-permute-start.7 = (f32[136,4]{1,0:T(8,128)S(1)}, f32[136,4]{1,0:T(8,128)S(1)}, u32[]{:S(2)}, u32[]{:S(2)}) collective-permute-start(f32[136,4]{1,0:T(8,128)S(1)} %get-tuple-element.180), channel_id=1, source_target_pairs={{1,0},{2,1},{3,2},{5,4},{6,5},{7,6},{9,8},{10,9},{11,10},{13,12},{... | collective-permute-start | bytes 6536 | tf_op jit(solution)/shard_map/ppermute | solution.py:53
  19.4 0.7 copy-start.13
  20.6 0.7 copy-start.11
  20.6 0.7 copy-start.12
  21.2 14.4 %copy-start.23 = (f32[2,2,128]{2,0,1:T(2,128)S(1)}, f32[2,2,128]{2,0,1:T(2,128)}, u32[]{:S(2)}) copy-start(f32[2,2,128]{2,0,1:T(2,128)} %constant.34.clone) | copy-start | bytes 6148
  21.3 5.0 %collective-permute-start = (f32[2,4,768]{2,1,0:T(4,128)S(1)}, f32[2,4,768]{2,1,0:T(4,128)S(1)}, u32[]{:S(2)}, u32[]{:S(2)}) collective-permute-start(f32[2,4,768]{2,1,0:T(4,128)S(1)} %maximum_add_fusion.8), channel_id=1, source_target_pairs={{0,1},{1,2},{2,3},{4,5},{5,6},{6,7},{8,9},{9,10},{10,11},{12,13},{... | collective-permute-start | bytes 73736 | tf_op jit(solution)/shard_map/while/body/eval_jaxpr/ppermute | solution.py:42
  26.4 4.6 %collective-permute-start = (f32[2,4,768]{2,1,0:T(4,128)S(1)}, f32[2,4,768]{2,1,0:T(4,128)S(1)}, u32[]{:S(2)}, u32[]{:S(2)}) collective-permute-start(f32[2,4,768]{2,1,0:T(4,128)S(1)} %maximum_add_fusion.8), channel_id=1, source_target_pairs={{0,1},{1,2},{2,3},{4,5},{5,6},{6,7},{8,9},{9,10},{10,11},{12,13},{... | collective-permute-start | bytes 73736 | tf_op jit(solution)/shard_map/while/body/eval_jaxpr/ppermute | solution.py:42
  31.1 4.6 %collective-permute-start = (f32[2,4,768]{2,1,0:T(4,128)S(1)}, f32[2,4,768]{2,1,0:T(4,128)S(1)}, u32[]{:S(2)}, u32[]{:S(2)}) collective-permute-start(f32[2,4,768]{2,1,0:T(4,128)S(1)} %maximum_add_fusion.8), channel_id=1, source_target_pairs={{0,1},{1,2},{2,3},{4,5},{5,6},{6,7},{8,9},{9,10},{10,11},{12,13},{... | collective-permute-start | bytes 73736 | tf_op jit(solution)/shard_map/while/body/eval_jaxpr/ppermute | solution.py:42
  36.5 0.7 copy-start.10
  37.1 14.0 %copy-start.22 = (f32[2,2,128]{2,0,1:T(2,128)S(1)}, f32[2,2,128]{2,0,1:T(2,128)}, u32[]{:S(2)}) copy-start(f32[2,2,128]{2,0,1:T(2,128)} %constant.36.clone) | copy-start | bytes 6148
  37.2 4.6 %collective-permute-start.1 = (f32[2,4,768]{2,1,0:T(4,128)S(1)}, f32[2,4,768]{2,1,0:T(4,128)S(1)}, u32[]{:S(2)}, u32[]{:S(2)}) collective-permute-start(f32[2,4,768]{2,1,0:T(4,128)S(1)} %maximum_add_fusion.9), channel_id=1, source_target_pairs={{1,0},{2,1},{3,2},{5,4},{6,5},{7,6},{9,8},{10,9},{11,10},{13,12},{... | collective-permute-start | bytes 73736 | tf_op jit(solution)/shard_map/while/body/eval_jaxpr/ppermute | solution.py:42
  41.9 4.6 %collective-permute-start.1 = (f32[2,4,768]{2,1,0:T(4,128)S(1)}, f32[2,4,768]{2,1,0:T(4,128)S(1)}, u32[]{:S(2)}, u32[]{:S(2)}) collective-permute-start(f32[2,4,768]{2,1,0:T(4,128)S(1)} %maximum_add_fusion.9), channel_id=1, source_target_pairs={{1,0},{2,1},{3,2},{5,4},{6,5},{7,6},{9,8},{10,9},{11,10},{13,12},{... | collective-permute-start | bytes 73736 | tf_op jit(solution)/shard_map/while/body/eval_jaxpr/ppermute | solution.py:42
  46.6 4.6 %collective-permute-start.1 = (f32[2,4,768]{2,1,0:T(4,128)S(1)}, f32[2,4,768]{2,1,0:T(4,128)S(1)}, u32[]{:S(2)}, u32[]{:S(2)}) collective-permute-start(f32[2,4,768]{2,1,0:T(4,128)S(1)} %maximum_add_fusion.9), channel_id=1, source_target_pairs={{1,0},{2,1},{3,2},{5,4},{6,5},{7,6},{9,8},{10,9},{11,10},{13,12},{... | collective-permute-start | bytes 73736 | tf_op jit(solution)/shard_map/while/body/eval_jaxpr/ppermute | solution.py:42
  51.1 0.8 copy-start.2
  52.0 0.7 copy-start.15
  53.0 0.7 copy-start.21
  53.7 0.8 copy-start.20
  54.5 0.8 copy-start.1
  55.3 0.7 copy-start.14
  56.4 0.7 copy-start.7
  56.4 0.7 copy-start.8
  57.2 11.0 %collective-permute-start.2 = (f32[2,4,768]{2,1,0:T(4,128)S(1)}, f32[2,4,768]{2,1,0:T(4,128)S(1)}, u32[]{:S(2)}, u32[]{:S(2)}) collective-permute-start(f32[2,4,768]{2,1,0:T(4,128)S(1)} %maximum_add_fusion.10), channel_id=1, source_target_pairs={{0,4},{4,8},{8,12},{12,16},{16,20},{20,24},{24,28},{1,5},{5,9},{9,... | collective-permute-start | bytes 73736 | tf_op jit(solution)/shard_map/while/body/eval_jaxpr/ppermute | solution.py:42
  68.3 6.0 %collective-permute-start.2 = (f32[2,4,768]{2,1,0:T(4,128)S(1)}, f32[2,4,768]{2,1,0:T(4,128)S(1)}, u32[]{:S(2)}, u32[]{:S(2)}) collective-permute-start(f32[2,4,768]{2,1,0:T(4,128)S(1)} %maximum_add_fusion.10), channel_id=1, source_target_pairs={{0,4},{4,8},{8,12},{12,16},{16,20},{20,24},{24,28},{1,5},{5,9},{9,... | collective-permute-start | bytes 73736 | tf_op jit(solution)/shard_map/while/body/eval_jaxpr/ppermute | solution.py:42
  74.4 6.0 %collective-permute-start.2 = (f32[2,4,768]{2,1,0:T(4,128)S(1)}, f32[2,4,768]{2,1,0:T(4,128)S(1)}, u32[]{:S(2)}, u32[]{:S(2)}) collective-permute-start(f32[2,4,768]{2,1,0:T(4,128)S(1)} %maximum_add_fusion.10), channel_id=1, source_target_pairs={{0,4},{4,8},{8,12},{12,16},{16,20},{20,24},{24,28},{1,5},{5,9},{9,... | collective-permute-start | bytes 73736 | tf_op jit(solution)/shard_map/while/body/eval_jaxpr/ppermute | solution.py:42
  80.5 6.0 %collective-permute-start.2 = (f32[2,4,768]{2,1,0:T(4,128)S(1)}, f32[2,4,768]{2,1,0:T(4,128)S(1)}, u32[]{:S(2)}, u32[]{:S(2)}) collective-permute-start(f32[2,4,768]{2,1,0:T(4,128)S(1)} %maximum_add_fusion.10), channel_id=1, source_target_pairs={{0,4},{4,8},{8,12},{12,16},{16,20},{20,24},{24,28},{1,5},{5,9},{9,... | collective-permute-start | bytes 73736 | tf_op jit(solution)/shard_map/while/body/eval_jaxpr/ppermute | solution.py:42
  86.7 6.0 %collective-permute-start.2 = (f32[2,4,768]{2,1,0:T(4,128)S(1)}, f32[2,4,768]{2,1,0:T(4,128)S(1)}, u32[]{:S(2)}, u32[]{:S(2)}) collective-permute-start(f32[2,4,768]{2,1,0:T(4,128)S(1)} %maximum_add_fusion.10), channel_id=1, source_target_pairs={{0,4},{4,8},{8,12},{12,16},{16,20},{20,24},{24,28},{1,5},{5,9},{9,... | collective-permute-start | bytes 73736 | tf_op jit(solution)/shard_map/while/body/eval_jaxpr/ppermute | solution.py:42
  92.8 6.0 %collective-permute-start.2 = (f32[2,4,768]{2,1,0:T(4,128)S(1)}, f32[2,4,768]{2,1,0:T(4,128)S(1)}, u32[]{:S(2)}, u32[]{:S(2)}) collective-permute-start(f32[2,4,768]{2,1,0:T(4,128)S(1)} %maximum_add_fusion.10), channel_id=1, source_target_pairs={{0,4},{4,8},{8,12},{12,16},{16,20},{20,24},{24,28},{1,5},{5,9},{9,... | collective-permute-start | bytes 73736 | tf_op jit(solution)/shard_map/while/body/eval_jaxpr/ppermute | solution.py:42
  98.9 6.0 %collective-permute-start.2 = (f32[2,4,768]{2,1,0:T(4,128)S(1)}, f32[2,4,768]{2,1,0:T(4,128)S(1)}, u32[]{:S(2)}, u32[]{:S(2)}) collective-permute-start(f32[2,4,768]{2,1,0:T(4,128)S(1)} %maximum_add_fusion.10), channel_id=1, source_target_pairs={{0,4},{4,8},{8,12},{12,16},{16,20},{20,24},{24,28},{1,5},{5,9},{9,... | collective-permute-start | bytes 73736 | tf_op jit(solution)/shard_map/while/body/eval_jaxpr/ppermute | solution.py:42
  105.0 0.7 copy-start.6
  105.8 6.6 %collective-permute-start.3 = (f32[2,4,768]{2,1,0:T(4,128)S(1)}, f32[2,4,768]{2,1,0:T(4,128)S(1)}, u32[]{:S(2)}, u32[]{:S(2)}) collective-permute-start(f32[2,4,768]{2,1,0:T(4,128)S(1)} %maximum_add_fusion.11), channel_id=1, source_target_pairs={{4,0},{8,4},{12,8},{16,12},{20,16},{24,20},{28,24},{5,1},{9,5},{13... | collective-permute-start | bytes 73736 | tf_op jit(solution)/shard_map/while/body/eval_jaxpr/ppermute | solution.py:42
  112.5 6.0 %collective-permute-start.3 = (f32[2,4,768]{2,1,0:T(4,128)S(1)}, f32[2,4,768]{2,1,0:T(4,128)S(1)}, u32[]{:S(2)}, u32[]{:S(2)}) collective-permute-start(f32[2,4,768]{2,1,0:T(4,128)S(1)} %maximum_add_fusion.11), channel_id=1, source_target_pairs={{4,0},{8,4},{12,8},{16,12},{20,16},{24,20},{28,24},{5,1},{9,5},{13... | collective-permute-start | bytes 73736 | tf_op jit(solution)/shard_map/while/body/eval_jaxpr/ppermute | solution.py:42
  118.6 6.0 %collective-permute-start.3 = (f32[2,4,768]{2,1,0:T(4,128)S(1)}, f32[2,4,768]{2,1,0:T(4,128)S(1)}, u32[]{:S(2)}, u32[]{:S(2)}) collective-permute-start(f32[2,4,768]{2,1,0:T(4,128)S(1)} %maximum_add_fusion.11), channel_id=1, source_target_pairs={{4,0},{8,4},{12,8},{16,12},{20,16},{24,20},{28,24},{5,1},{9,5},{13... | collective-permute-start | bytes 73736 | tf_op jit(solution)/shard_map/while/body/eval_jaxpr/ppermute | solution.py:42
  124.7 6.0 %collective-permute-start.3 = (f32[2,4,768]{2,1,0:T(4,128)S(1)}, f32[2,4,768]{2,1,0:T(4,128)S(1)}, u32[]{:S(2)}, u32[]{:S(2)}) collective-permute-start(f32[2,4,768]{2,1,0:T(4,128)S(1)} %maximum_add_fusion.11), channel_id=1, source_target_pairs={{4,0},{8,4},{12,8},{16,12},{20,16},{24,20},{28,24},{5,1},{9,5},{13... | collective-permute-start | bytes 73736 | tf_op jit(solution)/shard_map/while/body/eval_jaxpr/ppermute | solution.py:42
  130.9 6.0 %collective-permute-start.3 = (f32[2,4,768]{2,1,0:T(4,128)S(1)}, f32[2,4,768]{2,1,0:T(4,128)S(1)}, u32[]{:S(2)}, u32[]{:S(2)}) collective-permute-start(f32[2,4,768]{2,1,0:T(4,128)S(1)} %maximum_add_fusion.11), channel_id=1, source_target_pairs={{4,0},{8,4},{12,8},{16,12},{20,16},{24,20},{28,24},{5,1},{9,5},{13... | collective-permute-start | bytes 73736 | tf_op jit(solution)/shard_map/while/body/eval_jaxpr/ppermute | solution.py:42
  137.0 6.0 %collective-permute-start.3 = (f32[2,4,768]{2,1,0:T(4,128)S(1)}, f32[2,4,768]{2,1,0:T(4,128)S(1)}, u32[]{:S(2)}, u32[]{:S(2)}) collective-permute-start(f32[2,4,768]{2,1,0:T(4,128)S(1)} %maximum_add_fusion.11), channel_id=1, source_target_pairs={{4,0},{8,4},{12,8},{16,12},{20,16},{24,20},{28,24},{5,1},{9,5},{13... | collective-permute-start | bytes 73736 | tf_op jit(solution)/shard_map/while/body/eval_jaxpr/ppermute | solution.py:42
  143.2 6.0 %collective-permute-start.3 = (f32[2,4,768]{2,1,0:T(4,128)S(1)}, f32[2,4,768]{2,1,0:T(4,128)S(1)}, u32[]{:S(2)}, u32[]{:S(2)}) collective-permute-start(f32[2,4,768]{2,1,0:T(4,128)S(1)} %maximum_add_fusion.11), channel_id=1, source_target_pairs={{4,0},{8,4},{12,8},{16,12},{20,16},{24,20},{28,24},{5,1},{9,5},{13... | collective-permute-start | bytes 73736 | tf_op jit(solution)/shard_map/while/body/eval_jaxpr/ppermute | solution.py:42
  149.3 0.7 copy-start.19
  149.9 0.8 copy-start.18
  150.8 0.8 copy-start.17
  151.6 0.8 copy-start.16
  152.4 0.8 copy-start.4
  152.4 0.8 copy-start.25
  153.3 0.8 copy-start.3
  153.3 0.8 copy-start.24
  (2 other events, 1.3 us)
where the time goes:
time: 157 us; the launch traced here: 156 us
  starting transfers between devices  80.6 us (51%)
  waiting for transfers between devices  54.2 us (35%)
  matrix products  9.94 us (6%)
  local copies, waits for them, and re-layouts  7.83 us (5%)
  other arithmetic  2.56 us (2%)
    ppermute x20, starting transfers between devices, passed_along(): lax.ppermute(value, axis, [(source, source + steps) for source in range(l...  69.6 us
    ppermute x20, waiting for transfers between devices, passed_along(): lax.ppermute(value, axis, [(source, source + steps) for source in range(l...  48.2 us
    ppermute x2, starting transfers between devices, extended(): lax.ppermute(lax.slice_in_dim(block, block.shape[dim] - width, None, axis...  6.87 us
    ppermute x2, waiting for transfers between devices, extended(): lax.ppermute(lax.slice_in_dim(block, 0, width, axis=dim), axis, backward)  5.95 us
    unnamed x55, local copies, waits for them, and re-layouts  5.9 us
    ppermute x2, starting transfers between devices, extended(): lax.ppermute(lax.slice_in_dim(block, 0, width, axis=dim), axis, backward)  4.13 us
  transfers between devices with their start and end apart: 24, of which 22 were waited for; matrix products, arithmetic and copies ran while one was open for 1% of the time, Pallas kernels for 0%

commit v1 on v0

v1 whole, which is shorter than its diff:
```python
import math

import jax
import jax.numpy as jnp
import ml_dtypes
import numpy as np
from jax import lax
from jax.experimental import pallas as pl
from jax.experimental.pallas import tpu as pltpu
from jax.sharding import PartitionSpec as P

SIG_A = 128
SIG_B = 256
DEVIATIONS = (SIG_A, SIG_B)

DER_FIRST = (
    1.0 / 280,
    -4.0 / 105,
    1.0 / 5,
    -4.0 / 5,
    0.0,
    4.0 / 5,
    -1.0 / 5,
    4.0 / 105,
    -1.0 / 280,
)
DER_SECOND = (
    -1.0 / 560,
    8.0 / 315,
    -1.0 / 5,
    8.0 / 5,
    -205.0 / 72,
    8.0 / 5,
    -1.0 / 5,
    8.0 / 315,
    -1.0 / 560,
)
IDENTITY = (0.0, 0.0, 0.0, 0.0, 1.0, 0.0, 0.0, 0.0, 0.0)
STENCILS = (IDENTITY, DER_FIRST, DER_SECOND)
DERICHE_POLES = ((1.68, 3.735, 1.783, 0.6318), (-0.6803, -0.2598, 1.723, 1.997))
FEATURES = ((0, 0), (0, 1), (1, 0), (0, 2), (1, 1), (2, 0))

HALO = 4
CAUSAL, FIRST, LAST, ANTICAUSAL = 0, 8, 12, 16
BASIS = 24
SENT = 16
LANES = 128


def pole_values(deviation):
    normal_sum = 0.0
    for cos_weight, sin_weight, decay, freq in DERICHE_POLES:
        z = np.exp(complex(-decay, freq) / deviation)
        q = z / (1.0 - z)
        normal_sum += cos_weight + 2.0 * (cos_weight * q.real + sin_weight * q.imag)
    weights = [complex(cw, -sw) / normal_sum for cw, sw, _, _ in DERICHE_POLES]
    exponents = [complex(decay, -freq) / deviation for _, _, decay, freq in DERICHE_POLES]
    return np.array(weights), np.array(exponents)


def all_poles():
    return [pole_values(deviation) for deviation in DEVIATIONS]


def smooth_kernel(poles, distance):
    weights, exponents = poles
    return sum(
        (w * np.exp(-e * np.abs(distance))).real for w, e in zip(weights, exponents)
    )


def summary_table(length):
    cells = np.arange(length)
    table = np.zeros((BASIS, length))
    row = 0
    for _, exponents in all_poles():
        for e in exponents:
            causal = np.exp(-e * (length - 1 - cells))
            anticausal = np.exp(-e * cells)
            table[CAUSAL + row], table[CAUSAL + row + 1] = causal.real, causal.imag
            table[ANTICAUSAL + row], table[ANTICAUSAL + row + 1] = (
                anticausal.real,
                anticausal.imag,
            )
            row += 2
    for i in range(HALO):
        table[FIRST + i, i] = 1.0
        table[LAST + i, length - HALO + i] = 1.0
    return table


def cell_weight(poles, stencil, out_cells, in_cells, total):
    result = np.zeros((len(out_cells), len(in_cells)))
    for t in range(-HALO, HALO + 1):
        field_cells = in_cells - t
        inside = (field_cells >= 0) & (field_cells < total)
        distance = out_cells[:, None] - field_cells[None, :]
        result += stencil[t + HALO] * smooth_kernel(poles, distance) * inside[None, :]
    return result


def summary_weight(level, stencil, block, source, length, blocks):
    poles = all_poles()[level]
    weights, exponents = poles
    total = length * blocks
    out_cells = block * length + np.arange(length)
    after = block > source
    base = CAUSAL if after else FIRST
    offset = (CAUSAL if after else ANTICAUSAL) + 4 * level
    sign = 1.0 if after else -1.0
    anchor = source * length + (length - 1 if after else 0)
    table = np.zeros((length, BASIS))
    for p, (w, e) in enumerate(zip(weights, exponents)):
        eigen = sum(stencil[t + HALO] * np.exp(-sign * e * t) for t in range(-HALO, HALO + 1))
        gain = w * eigen * np.exp(-e * np.abs(out_cells - anchor))
        table[:, offset + 2 * p] = gain.real
        table[:, offset + 2 * p + 1] = -gain.imag

    def far_form(cells):
        result = np.zeros((length, len(cells)))
        for t in range(-HALO, HALO + 1):
            distance = sign * (out_cells[:, None] - (cells - t)[None, :])
            result += stencil[t + HALO] * sum(
                (w * np.exp(-e * distance)).real for w, e in zip(weights, exponents)
            )
        return result

    for position, start in ((FIRST, 0), (LAST, length - HALO)):
        cells = source * length + start + np.arange(HALO)
        at_end = (cells[0] == 0) or (cells[-1] == total - 1)
        adjacent = (cells[-1] + 1 == out_cells[0]) or (out_cells[-1] + 1 == cells[0])
        if at_end or adjacent:
            table[:, position : position + HALO] = cell_weight(
                poles, stencil, out_cells, cells, total
            ) - far_form(cells)
    return table[:, base : base + SENT]


def operator_tables(length, blocks, gains):
    remote = -(-SENT * blocks // LANES) * LANES
    tables = np.zeros((blocks, 2, 3, length, length + remote))
    for block in range(blocks):
        cells = block * length + np.arange(length)
        for level, poles in enumerate(all_poles()):
            for s, stencil in enumerate(STENCILS):
                view = tables[block, level, s]
                view[:, :length] = cell_weight(poles, stencil, cells, cells, length * blocks)
                for source in range(blocks):
                    if source != block:
                        start = length + SENT * source
                        view[:, start : start + SENT] = summary_weight(
                            level, stencil, block, source, length, blocks
                        )
                view *= gains[level][s]
    return tables


def window_tables(tables, length, blocks):
    middle = blocks // 2
    own = np.stack([tables[b, ..., :length] for b in (0, middle, blocks - 1)])
    inner = np.zeros((2 * blocks - 1,) + tables.shape[1:-1] + (SENT,))
    for block in range(blocks):
        for source in range(1, blocks - 1):
            start = length + SENT * source
            inner[source - block + blocks - 1] = tables[block, ..., start : start + SENT]
    ends = np.stack(
        [
            tables[..., length + SENT * end : length + SENT * (end + 1)]
            for end in (0, blocks - 1)
        ],
        axis=1,
    )

    def cells_first(table, lead):
        moved = np.moveaxis(table, -1, lead)
        return moved.reshape(moved.shape[: lead + 1] + (-1,))

    inner = cells_first(inner, 1)
    return (
        np.moveaxis(split_table(cells_first(own, 1)), 0, 1),
        split_table(inner.reshape(-1, inner.shape[-1])),
        np.moveaxis(split_table(cells_first(ends, 2)), 0, 2),
    )


def split_table(values):
    high = values.astype(ml_dtypes.bfloat16)
    low = (values - high.astype(np.float64)).astype(ml_dtypes.bfloat16)
    return np.stack([high, low])


def split(values):
    high = values.astype(jnp.bfloat16)
    low = (values - high.astype(jnp.float32)).astype(jnp.bfloat16)
    return high, low


def dot3(left, right, dims=((1,), (0,))):
    def dot(a, b):
        return lax.dot_general(a, b, (dims, ((), ())), preferred_element_type=jnp.float32)

    return dot(left[0], right[0]) + (dot(left[0], right[1]) + dot(left[1], right[0]))


NT = ((1,), (1,))


def summarize(
    rows, cols, image, sums, row_op, own_op, inner_op, ends_op, sent, block, row_own, col_own, tables, sems
):
    row, col = lax.axis_index("row"), lax.axis_index("col")
    width = image.shape[1]
    variant = jnp.where(col == 0, 0, jnp.where(col == cols - 1, 2, 1))
    window = pl.multiple_of(SENT * (cols - col), SENT)
    last = width + SENT * (cols - 1)

    def col_rows(start, count):
        return col_own.at[:, pl.ds(start, count)]

    pairs = [
        (image, block),
        (sums, tables),
        (row_op.at[row], row_own),
        (own_op.at[variant], col_rows(0, width)),
        (ends_op.at[col, 0], col_rows(width, SENT)),
        (
            inner_op.at[:, pl.ds(window, SENT * (cols - 2))],
            col_rows(width + SENT, SENT * (cols - 2)),
        ),
        (ends_op.at[col, 1], col_rows(last, SENT)),
    ]
    copies = [pltpu.make_async_copy(*pair, sems.at[i]) for i, pair in enumerate(pairs)]
    for copy in copies:
        copy.start()
    copies[0].wait()
    copies[1].wait()
    cells = split(block[...])
    row_sums = dot3((tables[0, 0], tables[0, 1]), cells)
    col_table = (tables[1, 0], tables[1, 1])
    col_sums = dot3(col_table, cells, NT)
    both = dot3(split(row_sums), col_table, NT)
    lane = lax.broadcasted_iota(jnp.int32, both.shape, 1)
    shift = SENT * lax.rem(col, LANES // SENT)
    ahead = pltpu.roll(jnp.where(lane < SENT, both, 0.0), shift, 1)
    back = pltpu.roll(both, LANES - FIRST, 1)
    back = pltpu.roll(jnp.where(lane < SENT, back, 0.0), shift, 1)

    def after(values):
        return values[CAUSAL : CAUSAL + SENT]

    def before(values):
        return values[FIRST : FIRST + SENT]

    for to_row in range(rows):
        row_after = to_row > row
        straight = jnp.where(row_after, after(row_sums), before(row_sums))
        right = jnp.where(row_after, after(ahead), before(ahead))
        left = jnp.where(row_after, after(back), before(back))
        for to_col in range(cols):
            across = jnp.where(to_col > col, after(col_sums), before(col_sums))
            corner = jnp.where(to_col > col, right, left)
            piece = jnp.where(to_col == col, straight, corner)
            sent[to_row * cols + to_col] = jnp.where(to_row == row, across, piece)
    rest = col_own.shape[1] - last - SENT
    if rest:
        col_own[:, last + SENT :] = jnp.zeros((2, rest, col_own.shape[2]), jnp.bfloat16)
    for copy in copies[2:]:
        copy.wait()


def combine(rows, cols, block, got, row_own, col_own, out, staged, sems):
    row, col = lax.axis_index("row"), lax.axis_index("col")
    length = block.shape[0]
    groups = -(-SENT * cols // LANES)
    fill = groups * LANES - SENT * cols
    across = got[pl.ds(row * cols, cols)].reshape(SENT * cols, length)
    if fill:
        across = jnp.concatenate([across, jnp.zeros((fill, length), jnp.float32)])
    upper = jnp.concatenate([block[...], across.T], axis=1)
    lower = []
    for from_row in range(rows):
        parts = [got[from_row * cols + col]]
        for group in range(groups):
            total = jnp.zeros((SENT, LANES), jnp.float32)
            for from_col in range(group * (LANES // SENT), min(cols, (group + 1) * (LANES // SENT))):
                total += jnp.where(from_col == col, 0.0, got[from_row * cols + from_col])
            parts.append(total)
        lower.append(jnp.concatenate(parts, axis=1))
    fill = -(-SENT * rows // LANES) * LANES - SENT * rows
    if fill:
        lower.append(jnp.zeros((fill, upper.shape[1]), jnp.float32))
    known = split(jnp.concatenate([upper] + lower))
    width = out.shape[2]
    copies = []
    for level in range(2):
        span = 3 * width
        smoothed = split(
            dot3(known, [col_own[i, :, span * level : span * (level + 1)] for i in range(2)])
        )
        for f, (row_stencil, col_stencil) in enumerate(FEATURES):
            columns = slice(width * col_stencil, width * (col_stencil + 1))
            feature = dot3(
                [row_own[i, level, row_stencil] for i in range(2)],
                [part[:, columns] for part in smoothed],
            )
            channel = len(FEATURES) * level + f
            staged[channel] = feature.astype(jnp.bfloat16)
            copies.append(
                pltpu.make_async_copy(staged.at[channel], out.at[channel], sems.at[channel])
            )
            copies[-1].start()
    for copy in copies:
        copy.wait()


def on_device(rows, cols, image):
    height, width = image.shape
    base = [2.0 * math.sqrt(math.pi) * s for s in DEVIATIONS]
    row_tables = operator_tables(
        height, rows, [[b * s**k for k in range(3)] for b, s in zip(base, DEVIATIONS)]
    )
    col_tables = operator_tables(width, cols, [[s**k for k in range(3)] for s in DEVIATIONS])
    row_op = np.moveaxis(split_table(row_tables), 0, 1)
    own_op, inner_op, ends_op = window_tables(col_tables, width, cols)
    col_own_shape = (2, col_tables.shape[-1], own_op.shape[-1])
    sums = np.zeros((2, 2, LANES, max(height, width)))
    sums[0, :, :BASIS, :height] = split_table(summary_table(height))
    sums[1, :, :BASIS, :width] = split_table(summary_table(width))
    sums = sums.astype(ml_dtypes.bfloat16)

    def in_vmem(count):
        return [pl.BlockSpec(memory_space=pltpu.VMEM)] * count

    params = pltpu.CompilerParams(vmem_limit_bytes=16 * 1024 * 1024)
    operands = [image] + [jnp.asarray(x) for x in (sums, row_op, own_op, inner_op, ends_op)]
    operands = [pltpu.with_memory_space_constraint(x, pltpu.HBM) for x in operands]
    sent, block, row_own, col_own = pl.pallas_call(
        lambda *refs: summarize(rows, cols, *refs),
        out_shape=[
            pltpu.VMEM((rows * cols, SENT, LANES), jnp.float32),
            pltpu.VMEM((height, width), jnp.float32),
            pltpu.VMEM(row_op.shape[1:], jnp.bfloat16),
            pltpu.VMEM(col_own_shape, jnp.bfloat16),
        ],
        in_specs=[pl.BlockSpec(memory_space=pltpu.HBM)] * len(operands),
        out_specs=in_vmem(4),
        scratch_shapes=[
            pltpu.VMEM(sums.shape, jnp.bfloat16),
            pltpu.SemaphoreType.DMA((7,)),
        ],
        compiler_params=params,
        name="summaries",
    )(*operands)
    got = lax.all_to_all(sent, ("row", "col"), 0, 0)
    features = 2 * len(FEATURES)
    return pl.pallas_call(
        lambda *refs: combine(rows, cols, *refs),
        out_shape=jax.ShapeDtypeStruct((features, height, width), jnp.bfloat16),
        in_specs=in_vmem(4),
        out_specs=pl.BlockSpec(memory_space=pl.ANY),
        scratch_shapes=[
            pltpu.VMEM((features, height, width), jnp.bfloat16),
            pltpu.SemaphoreType.DMA((features,)),
        ],
        compiler_params=params,
        name="combine",
    )(block, got, row_own, col_own)


def solution(mesh):
    rows, cols = mesh.shape["row"], mesh.shape["col"]
    return jax.shard_map(
        lambda image: on_device(rows, cols, image),
        mesh=mesh,
        in_specs=(P("row", "col"),),
        out_specs=P(None, "row", "col"),
        check_vma=False,
    )
```

time: 157 us -> 21.3 us (0.14)
  the two profiles are of different devices: /device:TPU:11 before, /device:TPU:0 now
where the time goes in v1:
time: 21.3 us; the launch traced here: 21.1 us
  blocking collectives  17.3 us (81%)
  Pallas kernels  3.79 us (18%)
    all_to_all x1, blocking collectives, on_device(): got = lax.all_to_all(sent, ('row', 'col'), 0, 0)  17.3 us
    pallas_call x1, Pallas kernels, on_device(): pl.pallas_call(lambda *refs: combine(rows, cols, *refs), out_shape=jax.Sh...  2.24 us
    pallas_call x1, Pallas kernels, on_device(): pl.pallas_call(lambda *refs: summarize(rows, cols, *refs), out_shape=[plt...  1.54 us

profile of v1, /device:TPU:0, one launch (start us, length us, event | category | flops | bytes accessed | tf_op | source)
XLA Modules:
  0.0 21.1 jit_solution(14009251443441113034)
XLA Ops:
  0.0 1.5 %summaries.1 = (f32[32,16,128]{2,1,0:T(8,128)S(1)}, f32[128,128]{1,0:T(8,128)S(1)}, bf16[2,2,3,128,256]{4,3,2,1,0:T(8,128)(2,1)S(1)}, bf16[2,256,768]{2,1,0:T(8,128)(2,1)S(1)}) custom-call(f32[128,128]{1,0:T(8,128)} %refs_0_.1, bf16[2,2,128,128]{3,2,1,0:T(8,128)(2,1)} %constant.10.clone.refs_1_, bf16[8,2,2,3,128,256]{5,4,3,2,1,0:T(8,128)(2,1)} %constant.11.clone.refs_2_, ...), custom_call_target="tpu_custom_call" | custom-call | tf_op jit(solution)/shard_map/summaries/pallas_call | solution.py:337
  1.6 17.3 %all_to_all.5.refs_1_ = f32[32,16,128]{2,1,0:T(8,128)S(1)} all-to-all(f32[32,16,128]{2,1,0:T(8,128)S(1)} %get-tuple-element.10), channel_id=1, replica_groups=mesh['row'=8,'col'=4] {'row','col'}, dimensions={0} | all-to-all | bytes 524288 | tf_op jit(solution)/shard_map/all_to_all | solution.py:354
  18.9 2.2 %combine.1 = bf16[12,128,128]{2,1,0:T(8,128)(2,1)} custom-call(f32[128,128]{1,0:T(8,128)S(1)} %get-tuple-element.9.refs_0_, f32[32,16,128]{2,1,0:T(8,128)S(1)} %all_to_all.5.refs_1_, bf16[2,2,3,128,256]{4,3,2,1,0:T(8,128)(2,1)S(1)} %get-tuple-element.11.refs_2_, bf16[2,256,768]{2,1,0:T(8,128)(2,1)S(1)} %get-tuple-element.12.refs_3_), custom_call_target="tpu_custom_call" | custom-call | tf_op jit(solution)/shard_map/combine/pallas_call | solution.py:356

commit v2 on v1

--- a/solution.py
+++ b/solution.py
@@ -196,10 +196,9 @@
 
 
 def dot3(left, right, dims=((1,), (0,))):
-    def dot(a, b):
-        return lax.dot_general(a, b, (dims, ((), ())), preferred_element_type=jnp.float32)
-
-    return dot(left[0], right[0]) + (dot(left[0], right[1]) + dot(left[1], right[0]))
+    left = jnp.concatenate([left[0], left[0], left[1]], axis=dims[0][0])
+    right = jnp.concatenate([right[0], right[1], right[0]], axis=dims[1][0])
+    return lax.dot_general(left, right, (dims, ((), ())), preferred_element_type=jnp.float32)
 
 
 NT = ((1,), (1,))
@@ -239,6 +238,8 @@
     col_table = (tables[1, 0], tables[1, 1])
     col_sums = dot3(col_table, cells, NT)
     both = dot3(split(row_sums), col_table, NT)
+    fill = jnp.zeros((both.shape[0], LANES - both.shape[1]), jnp.float32)
+    both = jnp.concatenate([both, fill], axis=1)
     lane = lax.broadcasted_iota(jnp.int32, both.shape, 1)
     shift = SENT * lax.rem(col, LANES // SENT)
     ahead = pltpu.roll(jnp.where(lane < SENT, both, 0.0), shift, 1)
@@ -292,17 +293,19 @@
     known = split(jnp.concatenate([upper] + lower))
     width = out.shape[2]
     copies = []
+    along_cols = dot3(known, [col_own[i] for i in range(2)])
     for level in range(2):
         span = 3 * width
-        smoothed = split(
-            dot3(known, [col_own[i, :, span * level : span * (level + 1)] for i in range(2)])
-        )
+        smoothed = split(along_cols[:, span * level : span * (level + 1)])
+        products = [
+            dot3(
+                [row_own[i, level, k] for i in range(2)],
+                [part[:, : (3 - k) * width] for part in smoothed],
+            )
+            for k in range(3)
+        ]
         for f, (row_stencil, col_stencil) in enumerate(FEATURES):
-            columns = slice(width * col_stencil, width * (col_stencil + 1))
-            feature = dot3(
-                [row_own[i, level, row_stencil] for i in range(2)],
-                [part[:, columns] for part in smoothed],
-            )
+            feature = products[row_stencil][:, width * col_stencil : width * (col_stencil + 1)]
             channel = len(FEATURES) * level + f
             staged[channel] = feature.astype(jnp.bfloat16)
             copies.append(
@@ -323,7 +326,7 @@
     row_op = np.moveaxis(split_table(row_tables), 0, 1)
     own_op, inner_op, ends_op = window_tables(col_tables, width, cols)
     col_own_shape = (2, col_tables.shape[-1], own_op.shape[-1])
-    sums = np.zeros((2, 2, LANES, max(height, width)))
+    sums = np.zeros((2, 2, 32, max(height, width)))
     sums[0, :, :BASIS, :height] = split_table(summary_table(height))
     sums[1, :, :BASIS, :width] = split_table(summary_table(width))
     sums = sums.astype(ml_dtypes.bfloat16)

time: 21.3 us -> 20.6 us (0.967)
  Pallas kernels: 3.79 us -> 3.15 us
    pallas_call x1, Pallas kernels: 2.24 us -> 1.77 us  [on_device(): pl.pallas_call(lambda *refs: combine(rows, cols, *refs), out_shape=jax.Sh...]
where the time goes in v2:
time: 20.6 us; the launch traced here: 20.5 us
  blocking collectives  17.3 us (84%)
  Pallas kernels  3.15 us (15%)
    all_to_all x1, blocking collectives, on_device(): got = lax.all_to_all(sent, ('row', 'col'), 0, 0)  17.3 us
    pallas_call x1, Pallas kernels, on_device(): pl.pallas_call(lambda *refs: combine(rows, cols, *refs), out_shape=jax.Sh...  1.77 us
    pallas_call x1, Pallas kernels, on_device(): pl.pallas_call(lambda *refs: summarize(rows, cols, *refs), out_shape=[plt...  1.38 us

profile of v2, /device:TPU:0, one launch (start us, length us, event | category | flops | bytes accessed | tf_op | source)
XLA Modules:
  0.0 20.5 jit_solution(12728800143266032628)
XLA Ops:
  0.0 1.4 %summaries.1 = (f32[32,16,128]{2,1,0:T(8,128)S(1)}, f32[128,128]{1,0:T(8,128)S(1)}, bf16[2,2,3,128,256]{4,3,2,1,0:T(8,128)(2,1)S(1)}, bf16[2,256,768]{2,1,0:T(8,128)(2,1)S(1)}) custom-call(f32[128,128]{1,0:T(8,128)} %refs_0_.1, bf16[2,2,32,128]{3,2,1,0:T(8,128)(2,1)} %constant.10.clone.refs_1_, bf16[8,2,2,3,128,256]{5,4,3,2,1,0:T(8,128)(2,1)} %constant.11.clone.refs_2_, ...), custom_call_target="tpu_custom_call" | custom-call | tf_op jit(solution)/shard_map/summaries/pallas_call | solution.py:340
  1.4 17.3 %all_to_all.5.refs_1_ = f32[32,16,128]{2,1,0:T(8,128)S(1)} all-to-all(f32[32,16,128]{2,1,0:T(8,128)S(1)} %get-tuple-element.10), channel_id=1, replica_groups=mesh['row'=8,'col'=4] {'row','col'}, dimensions={0} | all-to-all | bytes 524288 | tf_op jit(solution)/shard_map/all_to_all | solution.py:357
  18.7 1.8 %combine.1 = bf16[12,128,128]{2,1,0:T(8,128)(2,1)} custom-call(f32[128,128]{1,0:T(8,128)S(1)} %get-tuple-element.9.refs_0_, f32[32,16,128]{2,1,0:T(8,128)S(1)} %all_to_all.5.refs_1_, bf16[2,2,3,128,256]{4,3,2,1,0:T(8,128)(2,1)S(1)} %get-tuple-element.11.refs_2_, bf16[2,256,768]{2,1,0:T(8,128)(2,1)S(1)} %get-tuple-element.12.refs_3_), custom_call_target="tpu_custom_call" | custom-call | tf_op jit(solution)/shard_map/combine/pallas_call | solution.py:359

commit v3 on v2

--- a/solution.py
+++ b/solution.py
@@ -45,6 +45,9 @@
 BASIS = 24
 SENT = 16
 LANES = 128
+ROW_ROWS = 48
+COL_ROWS = 32
+PIECE = SENT // 2 + 1
 
 
 def pole_values(deviation):
@@ -99,16 +102,15 @@
     return result
 
 
-def summary_weight(level, stencil, block, source, length, blocks):
+def summary_weight(level, stencil, out_start, length, start, extent, total):
     poles = all_poles()[level]
     weights, exponents = poles
-    total = length * blocks
-    out_cells = block * length + np.arange(length)
-    after = block > source
+    out_cells = out_start + np.arange(length)
+    after = out_start > start
     base = CAUSAL if after else FIRST
     offset = (CAUSAL if after else ANTICAUSAL) + 4 * level
     sign = 1.0 if after else -1.0
-    anchor = source * length + (length - 1 if after else 0)
+    anchor = start + (extent - 1 if after else 0)
     table = np.zeros((length, BASIS))
     for p, (w, e) in enumerate(zip(weights, exponents)):
         eigen = sum(stencil[t + HALO] * np.exp(-sign * e * t) for t in range(-HALO, HALO + 1))
@@ -125,8 +127,8 @@
             )
         return result
 
-    for position, start in ((FIRST, 0), (LAST, length - HALO)):
-        cells = source * length + start + np.arange(HALO)
+    for position, first in ((FIRST, start), (LAST, start + extent - HALO)):
+        cells = first + np.arange(HALO)
         at_end = (cells[0] == 0) or (cells[-1] == total - 1)
         adjacent = (cells[-1] + 1 == out_cells[0]) or (out_cells[-1] + 1 == cells[0])
         if at_end or adjacent:
@@ -136,22 +138,23 @@
     return table[:, base : base + SENT]
 
 
-def operator_tables(length, blocks, gains):
-    remote = -(-SENT * blocks // LANES) * LANES
+def operator_tables(length, blocks, sources, gains):
+    remote = -(-SENT * len(sources(0)) // LANES) * LANES
     tables = np.zeros((blocks, 2, 3, length, length + remote))
+    total = length * blocks
     for block in range(blocks):
         cells = block * length + np.arange(length)
         for level, poles in enumerate(all_poles()):
-            for s, stencil in enumerate(STENCILS):
-                view = tables[block, level, s]
-                view[:, :length] = cell_weight(poles, stencil, cells, cells, length * blocks)
-                for source in range(blocks):
-                    if source != block:
-                        start = length + SENT * source
-                        view[:, start : start + SENT] = summary_weight(
-                            level, stencil, block, source, length, blocks
+            for k, stencil in enumerate(STENCILS):
+                view = tables[block, level, k]
+                view[:, :length] = cell_weight(poles, stencil, cells, cells, total)
+                for place, source in enumerate(sources(block)):
+                    if source is not None:
+                        at = length + SENT * place
+                        view[:, at : at + SENT] = summary_weight(
+                            level, stencil, cells[0], length, *source, total
                         )
-                view *= gains[level][s]
+                view *= gains[level][k]
     return tables
 
 
@@ -204,10 +207,27 @@
 NT = ((1,), (1,))
 
 
-def summarize(
-    rows, cols, image, sums, row_op, own_op, inner_op, ends_op, sent, block, row_own, col_own, tables, sems
+def prepare(
+    cols,
+    image,
+    row_sums,
+    col_sums,
+    row_op,
+    own_op,
+    inner_op,
+    ends_op,
+    block,
+    row_own,
+    col_own,
+    other_table,
+    col_table,
+    by_rows,
+    by_cols,
+    own_table,
+    sems,
 ):
     row, col = lax.axis_index("row"), lax.axis_index("col")
+    half = lax.rem(row, 2)
     width = image.shape[1]
     variant = jnp.where(col == 0, 0, jnp.where(col == cols - 1, 2, 1))
     window = pl.multiple_of(SENT * (cols - col), SENT)
@@ -218,7 +238,9 @@
 
     pairs = [
         (image, block),
-        (sums, tables),
+        (row_sums.at[half], own_table),
+        (col_sums, col_table),
+        (row_sums.at[1 - half], other_table),
         (row_op.at[row], row_own),
         (own_op.at[variant], col_rows(0, width)),
         (ends_op.at[col, 0], col_rows(width, SENT)),
@@ -231,72 +253,151 @@
     copies = [pltpu.make_async_copy(*pair, sems.at[i]) for i, pair in enumerate(pairs)]
     for copy in copies:
         copy.start()
-    copies[0].wait()
-    copies[1].wait()
+    for copy in copies[:3]:
+        copy.wait()
     cells = split(block[...])
-    row_sums = dot3((tables[0, 0], tables[0, 1]), cells)
-    col_table = (tables[1, 0], tables[1, 1])
-    col_sums = dot3(col_table, cells, NT)
-    both = dot3(split(row_sums), col_table, NT)
-    fill = jnp.zeros((both.shape[0], LANES - both.shape[1]), jnp.float32)
-    both = jnp.concatenate([both, fill], axis=1)
-    lane = lax.broadcasted_iota(jnp.int32, both.shape, 1)
-    shift = SENT * lax.rem(col, LANES // SENT)
-    ahead = pltpu.roll(jnp.where(lane < SENT, both, 0.0), shift, 1)
-    back = pltpu.roll(both, LANES - FIRST, 1)
-    back = pltpu.roll(jnp.where(lane < SENT, back, 0.0), shift, 1)
-
-    def after(values):
-        return values[CAUSAL : CAUSAL + SENT]
-
-    def before(values):
-        return values[FIRST : FIRST + SENT]
-
-    for to_row in range(rows):
-        row_after = to_row > row
-        straight = jnp.where(row_after, after(row_sums), before(row_sums))
-        right = jnp.where(row_after, after(ahead), before(ahead))
-        left = jnp.where(row_after, after(back), before(back))
-        for to_col in range(cols):
-            across = jnp.where(to_col > col, after(col_sums), before(col_sums))
-            corner = jnp.where(to_col > col, right, left)
-            piece = jnp.where(to_col == col, straight, corner)
-            sent[to_row * cols + to_col] = jnp.where(to_row == row, across, piece)
+    by_rows[...] = dot3([own_table[i] for i in range(2)], cells)
+    by_cols[...] = dot3([col_table[i, :COL_ROWS] for i in range(2)], cells, NT)
     rest = col_own.shape[1] - last - SENT
     if rest:
         col_own[:, last + SENT :] = jnp.zeros((2, rest, col_own.shape[2]), jnp.bfloat16)
-    for copy in copies[2:]:
+    for copy in copies[3:]:
         copy.wait()
 
 
-def combine(rows, cols, block, got, row_own, col_own, out, staged, sems):
+def after(values):
+    return values[CAUSAL : CAUSAL + SENT]
+
+
+def before(values):
+    return values[FIRST : FIRST + SENT]
+
+
+def lane_place(shape):
+    return lax.broadcasted_iota(jnp.int32, shape, 1) // SENT
+
+
+def pack(rows, cols, other, other_table, col_table, by_rows, by_cols, sent, near):
     row, col = lax.axis_index("row"), lax.axis_index("col")
-    length = block.shape[0]
+    chip, half = row // 2, lax.rem(row, 2)
+    cells = split(other[...])
+    own_rows = by_rows[...]
+    other_rows = dot3([other_table[i] for i in range(2)], cells)
+    other_cols = dot3([col_table[i, :COL_ROWS] for i in range(2)], cells, NT)
+    near[...] = other_rows[BASIS : BASIS + SENT]
+    over_rows = own_rows[:BASIS] + other_rows[:BASIS]
+    own_near, other_near = own_rows[BASIS : BASIS + SENT], near[...]
+    own_cols = by_cols[...]
+    is_first = half == 0
+    nears = [
+        jnp.where(is_first, own_near, other_near),
+        jnp.where(is_first, other_near, own_near),
+    ]
+    over_cols = [
+        jnp.where(is_first, own_cols, other_cols),
+        jnp.where(is_first, other_cols, own_cols),
+    ]
+    corners = dot3(
+        split(jnp.concatenate([over_rows] + nears)),
+        [col_table[i, COL_ROWS:] for i in range(2)],
+        NT,
+    )
+
+    def share(values):
+        return jnp.where(is_first, values[: SENT // 2], values[SENT // 2 :])
+
+    straight = [share(after(over_rows)), share(before(over_rows))]
+    across, flat, placed = [], [], []
+    for to_half in range(2):
+        across.append([share(after(over_cols[to_half])), share(before(over_cols[to_half]))])
+    for side in range(2):
+        tiled = corners[:, LANES * side : LANES * (side + 1)]
+        mine = lane_place(tiled.shape) == lax.rem(col, LANES // SENT)
+        masked = jnp.where(mine, tiled, 0.0)
+        placed.append([share(after(masked)), share(before(masked))])
+        lines = []
+        for to_half in range(2):
+            start = BASIS + SENT * (1 - to_half)
+            part = share(tiled[start : start + SENT])
+            diagonal = lane_place(part.shape) == lax.broadcasted_iota(jnp.int32, part.shape, 0)
+            lines.append(jnp.sum(jnp.where(diagonal, part, 0.0), axis=0, keepdims=True))
+        flat.append(lines)
+    none = jnp.zeros((1, LANES), jnp.float32)
+    for to_chip in range(rows // 2):
+        is_after = to_chip > chip
+        is_here = to_chip == chip
+        line = jnp.where(is_after, straight[0], straight[1])
+        sides = [jnp.where(is_after, *placed[side]) for side in range(2)]
+        for to_half in range(2):
+            for to_col in range(cols):
+                is_right = to_col > col
+                body = jnp.where(to_col == col, line, jnp.where(is_right, *sides))
+                body = jnp.where(is_here, jnp.where(is_right, *across[to_half]), body)
+                tail = jnp.where(is_right, flat[0][to_half], flat[1][to_half])
+                at = PIECE * ((2 * to_chip + to_half) * cols + to_col)
+                sent[at : at + PIECE - 1] = body
+                sent[at + PIECE - 1 : at + PIECE] = jnp.where(is_here, tail, none)
+
+
+def combine(rows, cols, block, got, near, row_own, col_own, out, staged, sems):
+    row, col = lax.axis_index("row"), lax.axis_index("col")
+    chip = row // 2
+    length, width = block.shape
     groups = -(-SENT * cols // LANES)
-    fill = groups * LANES - SENT * cols
-    across = got[pl.ds(row * cols, cols)].reshape(SENT * cols, length)
-    if fill:
-        across = jnp.concatenate([across, jnp.zeros((fill, length), jnp.float32)])
-    upper = jnp.concatenate([block[...], across.T], axis=1)
-    lower = []
-    for from_row in range(rows):
-        parts = [got[from_row * cols + col]]
-        for group in range(groups):
-            total = jnp.zeros((SENT, LANES), jnp.float32)
-            for from_col in range(group * (LANES // SENT), min(cols, (group + 1) * (LANES // SENT))):
-                total += jnp.where(from_col == col, 0.0, got[from_row * cols + from_col])
-            parts.append(total)
-        lower.append(jnp.concatenate(parts, axis=1))
-    fill = -(-SENT * rows // LANES) * LANES - SENT * rows
-    if fill:
-        lower.append(jnp.zeros((fill, upper.shape[1]), jnp.float32))
+    per_group = LANES // SENT
+    nothing = jnp.zeros((SENT, LANES), jnp.float32)
+    half_shape = (SENT // 2, LANES)
+    diagonal = lane_place(half_shape) == lax.broadcasted_iota(jnp.int32, half_shape, 0)
+
+    def piece(from_chip, from_col):
+        ats = [PIECE * ((2 * from_chip + half) * cols + from_col) for half in range(2)]
+        return jnp.concatenate([got[at : at + PIECE - 1] for at in ats])
+
+    def corner(from_chip, from_col):
+        ats = [PIECE * ((2 * from_chip + half) * cols + from_col) for half in range(2)]
+        tails = [got[at + PIECE - 1 : at + PIECE] for at in ats]
+        return jnp.concatenate([jnp.where(diagonal, tail, 0.0) for tail in tails])
+
+    across, lower = [], []
+    corners = [nothing] * groups
+    pieces = [[piece(i, j) for j in range(cols)] for i in range(rows // 2)]
+    for from_col in range(cols):
+        here = nothing
+        tail = nothing
+        for from_chip in range(rows // 2):
+            here = jnp.where(from_chip == chip, pieces[from_chip][from_col], here)
+            tail = jnp.where(from_chip == chip, corner(from_chip, from_col), tail)
+        across.append(here)
+        shift = LANES // 2
+        while shift >= SENT:
+            tail = tail + pltpu.roll(tail, shift, 1)
+            shift //= 2
+        wanted = (lane_place(tail.shape) == from_col % per_group) & (from_col != col)
+        corners[from_col // per_group] += jnp.where(wanted, tail, 0.0)
+    if groups * per_group > cols:
+        across.append(jnp.zeros((groups * LANES - SENT * cols, length), jnp.float32))
+    upper = jnp.concatenate([block[...], jnp.concatenate(across).T], axis=1)
+    for from_chip in range(rows // 2):
+        is_here = from_chip == chip
+        line = near[...]
+        parts = [jnp.where(is_here, corner_sum, 0.0) for corner_sum in corners]
+        for from_col in range(cols):
+            found = pieces[from_chip][from_col]
+            is_col = from_col == col
+            line = jnp.where(jnp.logical_not(is_here) & is_col, found, line)
+            group = from_col // per_group
+            parts[group] += jnp.where(is_here | is_col, 0.0, found)
+        lower.append(jnp.concatenate([line] + parts, axis=1))
     known = split(jnp.concatenate([upper] + lower))
-    width = out.shape[2]
+    along_cols = dot3(known, [col_own[i] for i in range(2)])
+    fill = row_own.shape[-1] - along_cols.shape[0]
     copies = []
-    along_cols = dot3(known, [col_own[i] for i in range(2)])
     for level in range(2):
         span = 3 * width
         smoothed = split(along_cols[:, span * level : span * (level + 1)])
+        if fill:
+            rest = jnp.zeros((fill, span), jnp.bfloat16)
+            smoothed = [jnp.concatenate([part, rest]) for part in smoothed]
         products = [
             dot3(
                 [row_own[i, level, k] for i in range(2)],
@@ -316,50 +417,94 @@
         copy.wait()
 
 
+def row_tables(height, rows):
+    def sources(block):
+        chips = [(2 * height * chip, 2 * height) for chip in range(rows // 2)]
+        chips[block // 2] = ((block ^ 1) * height, height)
+        return chips
+
+    base = [2.0 * math.sqrt(math.pi) * s for s in DEVIATIONS]
+    gains = [[b * s**k for k in range(3)] for b, s in zip(base, DEVIATIONS)]
+    whole, single = summary_table(2 * height), summary_table(height)
+    sums = np.zeros((2, ROW_ROWS, height))
+    for half, own in enumerate((after(single), before(single))):
+        sums[half, :BASIS] = whole[:, half * height : (half + 1) * height]
+        sums[half, BASIS : BASIS + SENT] = own
+    return operator_tables(height, rows, sources, gains), sums
+
+
+def col_tables(width, cols):
+    def sources(block):
+        return [None if b == block else (b * width, width) for b in range(cols)]
+
+    gains = [[s**k for k in range(3)] for s in DEVIATIONS]
+    single = summary_table(width)
+    sums = np.zeros((COL_ROWS + 2 * LANES, width))
+    sums[:BASIS] = single
+    sums[COL_ROWS:] = np.concatenate(
+        [np.tile(part, (LANES // SENT, 1)) for part in (after(single), before(single))]
+    )
+    return operator_tables(width, cols, sources, gains), sums
+
+
 def on_device(rows, cols, image):
     height, width = image.shape
-    base = [2.0 * math.sqrt(math.pi) * s for s in DEVIATIONS]
-    row_tables = operator_tables(
-        height, rows, [[b * s**k for k in range(3)] for b, s in zip(base, DEVIATIONS)]
-    )
-    col_tables = operator_tables(width, cols, [[s**k for k in range(3)] for s in DEVIATIONS])
-    row_op = np.moveaxis(split_table(row_tables), 0, 1)
-    own_op, inner_op, ends_op = window_tables(col_tables, width, cols)
-    col_own_shape = (2, col_tables.shape[-1], own_op.shape[-1])
-    sums = np.zeros((2, 2, 32, max(height, width)))
-    sums[0, :, :BASIS, :height] = split_table(summary_table(height))
-    sums[1, :, :BASIS, :width] = split_table(summary_table(width))
-    sums = sums.astype(ml_dtypes.bfloat16)
+    row_weights, row_sums = row_tables(height, rows)
+    col_weights, col_sums = col_tables(width, cols)
+    row_op = np.moveaxis(split_table(row_weights), 0, 1)
+    col_ops = window_tables(col_weights, width, cols)
+    row_sums = np.moveaxis(split_table(row_sums), 0, 1)
+    col_sums = split_table(col_sums)
 
     def in_vmem(count):
         return [pl.BlockSpec(memory_space=pltpu.VMEM)] * count
 
     params = pltpu.CompilerParams(vmem_limit_bytes=16 * 1024 * 1024)
-    operands = [image] + [jnp.asarray(x) for x in (sums, row_op, own_op, inner_op, ends_op)]
-    operands = [pltpu.with_memory_space_constraint(x, pltpu.HBM) for x in operands]
-    sent, block, row_own, col_own = pl.pallas_call(
-        lambda *refs: summarize(rows, cols, *refs),
+    operands = [jnp.asarray(x) for x in (row_sums, col_sums, row_op, *col_ops)]
+    operands = [pltpu.with_memory_space_constraint(x, pltpu.HBM) for x in [image] + operands]
+    other = lax.ppermute(image, "row", [(i, i ^ 1) for i in range(rows)])
+    block, row_own, col_own, other_table, col_table, by_rows, by_cols = pl.pallas_call(
+        lambda *refs: prepare(cols, *refs),
         out_shape=[
-            pltpu.VMEM((rows * cols, SENT, LANES), jnp.float32),
             pltpu.VMEM((height, width), jnp.float32),
             pltpu.VMEM(row_op.shape[1:], jnp.bfloat16),
-            pltpu.VMEM(col_own_shape, jnp.bfloat16),
+            pltpu.VMEM((2, col_weights.shape[-1], 6 * width), jnp.bfloat16),
+            pltpu.VMEM(row_sums.shape[1:], jnp.bfloat16),
+            pltpu.VMEM(col_sums.shape, jnp.bfloat16),
+            pltpu.VMEM((ROW_ROWS, width), jnp.float32),
+            pltpu.VMEM((COL_ROWS, height), jnp.float32),
         ],
         in_specs=[pl.BlockSpec(memory_space=pltpu.HBM)] * len(operands),
-        out_specs=in_vmem(4),
+        out_specs=in_vmem(7),
         scratch_shapes=[
-            pltpu.VMEM(sums.shape, jnp.bfloat16),
-            pltpu.SemaphoreType.DMA((7,)),
+            pltpu.VMEM(row_sums.shape[1:], jnp.bfloat16),
+            pltpu.SemaphoreType.DMA((9,)),
         ],
         compiler_params=params,
-        name="summaries",
+        cost_estimate=pl.CostEstimate(
+            flops=6 * (ROW_ROWS + COL_ROWS) * height * width,
+            bytes_accessed=4 * 1024 * 1024,
+            transcendentals=0,
+        ),
+        name="prepare",
     )(*operands)
-    got = lax.all_to_all(sent, ("row", "col"), 0, 0)
+    sent, near = pl.pallas_call(
+        lambda *refs: pack(rows, cols, *refs),
+        out_shape=[
+            pltpu.VMEM((PIECE * rows * cols, LANES), jnp.float32),
+            pltpu.VMEM((SENT, width), jnp.float32),
+        ],
+        in_specs=in_vmem(5),
+        out_specs=in_vmem(2),
+        compiler_params=params,
+        name="pack",
+    )(other, other_table, col_table, by_rows, by_cols)
+    got = lax.all_to_all(sent.reshape(rows * cols, PIECE, 1, LANES), ("row", "col"), 0, 0)
     features = 2 * len(FEATURES)
     return pl.pallas_call(
         lambda *refs: combine(rows, cols, *refs),
         out_shape=jax.ShapeDtypeStruct((features, height, width), jnp.bfloat16),
-        in_specs=in_vmem(4),
+        in_specs=in_vmem(5),
         out_specs=pl.BlockSpec(memory_space=pl.ANY),
         scratch_shapes=[
             pltpu.VMEM((features, height, width), jnp.bfloat16),
@@ -367,7 +512,7 @@
         ],
         compiler_params=params,
         name="combine",
-    )(block, got, row_own, col_own)
+    )(block, got.reshape(sent.shape), near, row_own, col_own)
 
 
 def solution(mesh):

time: 20.6 us -> 19.7 us (0.956)
  blocking collectives: 17.3 us -> 15.4 us
  Pallas kernels: 3.15 us -> 3.66 us
  starting transfers between devices: 0 us -> 0.45 us
    all_to_all x1, blocking collectives: 17.3 us -> 15.4 us  [on_device(): lax.all_to_all(sent.reshape(rows * cols, PIECE, 1, LANES), ('row', 'col')...]
    ppermute x0 -> x1, starting transfers between devices: none -> 0.45 us  [on_device(): other = lax.ppermute(image, 'row', [(i, i ^ 1) for i in range(rows)])]
    pallas_call x1 -> x2, Pallas kernels: 1.38 us -> 1.82 us  [the longest x1 1.49 us: on_device(): pl.pallas_call(lambda *refs: prepare(cols, *refs), out_shape=[pltpu.VMEM(...]
  transfers between devices with their start and end apart: 0 -> 1, of which waited for: 0 -> 0; matrix products, arithmetic and copies ran while one was open for 0% -> 0% of each run, Pallas kernels for 0% -> 8%
where the time goes in v3:
time: 19.7 us; the launch traced here: 19.5 us
  blocking collectives  15.4 us (78%)
  Pallas kernels  3.66 us (19%)
  starting transfers between devices  0.45 us (2%)
    all_to_all x1, blocking collectives, on_device(): lax.all_to_all(sent.reshape(rows * cols, PIECE, 1, LANES), ('row', 'col')...  15.4 us
    pallas_call x1, Pallas kernels, on_device(): pl.pallas_call(lambda *refs: combine(rows, cols, *refs), out_shape=jax.Sh...  1.83 us
    pallas_call x1, Pallas kernels, on_device(): pl.pallas_call(lambda *refs: prepare(cols, *refs), out_shape=[pltpu.VMEM(...  1.49 us
    ppermute x1, starting transfers between devices, on_device(): other = lax.ppermute(image, 'row', [(i, i ^ 1) for i in range(rows)])  0.45 us
  transfers between devices with their start and end apart: 1, of which 0 were waited for; matrix products, arithmetic and copies ran while one was open for 0% of the time, Pallas kernels for 8%

profile of v3, /device:TPU:0, one launch (start us, length us, event | category | flops | bytes accessed | tf_op | source)
XLA Modules:
  0.0 19.5 jit_solution(605542682511262627)
XLA Ops:
  0.0 0.5 %collective-permute-start = (f32[128,128]{1,0:T(8,128)}, f32[128,128]{1,0:T(8,128)S(1)}, u32[]{:S(2)}, u32[]{:S(2)}) collective-permute-start(f32[128,128]{1,0:T(8,128)} %refs_0_.1), channel_id=1, source_target_pairs={{0,4},{4,0},{8,12},{12,8},{16,20},{20,16},{24,28},{28,24},{1,5},{5... | collective-permute-start | bytes 196616 | tf_op jit(solution)/shard_map/ppermute | solution.py:465
  0.5 1.5 %prepare.1 = (f32[128,128]{1,0:T(8,128)S(1)}, bf16[2,2,3,128,256]{4,3,2,1,0:T(8,128)(2,1)S(1)}, bf16[2,256,768]{2,1,0:T(8,128)(2,1)S(1)}, bf16[2,48,128]{2,1,0:T...) custom-call(f32[128,128]{1,0:T(8,128)} %refs_0_.1, ...), custom_call_target="tpu_custom_call" | custom-call | flops 7864320 | bytes 4194304 | tf_op jit(solution)/shard_map/prepare/pallas_call | solution.py:466
  1.9 0.0 collective-permute-done.refs_0_
  2.0 0.3 %pack.1 = (f32[288,128]{1,0:T(8,128)S(1)}, f32[16,128]{1,0:T(8,128)S(1)}) custom-call(f32[128,128]{1,0:T(8,128)S(1)} %collective-permute-done.refs_0_, bf16[2,48,128]{2,1,0:T(8,128)(2,1)S(1)} %get-tuple-element.15.refs_1_, bf16[2,288,128]{2,1,0:T(8,128)(2,1)S(1)} %get-tuple-element.16.refs_2_, f32[48,128]{1,0:T(8,128)S(1)} %get-tuple-element.17.refs_3_, ...), custom_call_target="tpu_custom_call" | custom-call | tf_op jit(solution)/shard_map/pack/pallas_call | solution.py:491
  2.3 15.4 %all_to_all.5 = f32[32,9,1,128]{3,2,1,0:T(1,128)S(1)} all-to-all(f32[32,9,1,128]{3,2,1,0:T(1,128)S(1)} %bitcast.3), channel_id=1, replica_groups=mesh['row'=8,'col'=4] {'row','col'}, dimensions={0} | all-to-all | bytes 294912 | tf_op jit(solution)/shard_map/all_to_all | solution.py:502
  17.7 1.8 %combine.1 = bf16[12,128,128]{2,1,0:T(8,128)(2,1)} custom-call(f32[128,128]{1,0:T(8,128)S(1)} %get-tuple-element.14.refs_0_, f32[288,128]{1,0:T(8,128)S(1)} %bitcast.2, f32[16,128]{1,0:T(8,128)S(1)} %get-tuple-element.20.refs_2_, bf16[2,2,3,128,256]{4,3,2,1,0:T(8,128)(2,1)S(1)} %get-tuple-element.21.refs_3_, bf16[2,256,768]{2,1,0:T(8,128)(2,1)S(1)} %get-tuple-element.22.refs_4_), custom_call_target="tpu_custom_call" | custom-call | tf_op jit(solution)/shard_map/combine/pallas_call | solution.py:504
Async XLA Ops:
  0.0 2.0 %collective-permute-start = (f32[128,128]{1,0:T(8,128)}, f32[128,128]{1,0:T(8,128)S(1)}, u32[]{:S(2)}, u32[]{:S(2)}) collective-permute-start(f32[128,128]{1,0:T(8,128)} %refs_0_.1), channel_id=1, source_target_pairs={{0,4},{4,0},{8,12},{12,8},{16,20},{20,16},{24,28},{28,24},{1,5},{5... | collective-permute-start | bytes 196616 | tf_op jit(solution)/shard_map/ppermute | solution.py:465

commit v4 on v3

--- a/solution.py
+++ b/solution.py
@@ -265,6 +265,14 @@
         copy.wait()
 
 
+def exchange_order(rows, cols):
+    def place(device):
+        row, col = divmod(device, cols)
+        return col % 2, row % 2, col // 2, row // 2
+
+    return sorted(range(rows * cols), key=place)
+
+
 def after(values):
     return values[CAUSAL : CAUSAL + SENT]
 
@@ -323,6 +331,7 @@
             lines.append(jnp.sum(jnp.where(diagonal, part, 0.0), axis=0, keepdims=True))
         flat.append(lines)
     none = jnp.zeros((1, LANES), jnp.float32)
+    order = exchange_order(rows, cols)
     for to_chip in range(rows // 2):
         is_after = to_chip > chip
         is_here = to_chip == chip
@@ -334,7 +343,7 @@
                 body = jnp.where(to_col == col, line, jnp.where(is_right, *sides))
                 body = jnp.where(is_here, jnp.where(is_right, *across[to_half]), body)
                 tail = jnp.where(is_right, flat[0][to_half], flat[1][to_half])
-                at = PIECE * ((2 * to_chip + to_half) * cols + to_col)
+                at = PIECE * order.index((2 * to_chip + to_half) * cols + to_col)
                 sent[at : at + PIECE - 1] = body
                 sent[at + PIECE - 1 : at + PIECE] = jnp.where(is_here, tail, none)
 
@@ -345,16 +354,21 @@
     length, width = block.shape
     groups = -(-SENT * cols // LANES)
     per_group = LANES // SENT
+    order = exchange_order(rows, cols)
     nothing = jnp.zeros((SENT, LANES), jnp.float32)
     half_shape = (SENT // 2, LANES)
     diagonal = lane_place(half_shape) == lax.broadcasted_iota(jnp.int32, half_shape, 0)
 
+    def places(from_chip, from_col):
+        devices = [(2 * from_chip + half) * cols + from_col for half in range(2)]
+        return [PIECE * order.index(device) for device in devices]
+
     def piece(from_chip, from_col):
-        ats = [PIECE * ((2 * from_chip + half) * cols + from_col) for half in range(2)]
+        ats = places(from_chip, from_col)
         return jnp.concatenate([got[at : at + PIECE - 1] for at in ats])
 
     def corner(from_chip, from_col):
-        ats = [PIECE * ((2 * from_chip + half) * cols + from_col) for half in range(2)]
+        ats = places(from_chip, from_col)
         tails = [got[at + PIECE - 1 : at + PIECE] for at in ats]
         return jnp.concatenate([jnp.where(diagonal, tail, 0.0) for tail in tails])
 
@@ -499,7 +513,13 @@
         compiler_params=params,
         name="pack",
     )(other, other_table, col_table, by_rows, by_cols)
-    got = lax.all_to_all(sent.reshape(rows * cols, PIECE, 1, LANES), ("row", "col"), 0, 0)
+    got = lax.all_to_all(
+        sent.reshape(rows * cols, PIECE, 1, LANES),
+        ("row", "col"),
+        0,
+        0,
+        axis_index_groups=[exchange_order(rows, cols)],
+    )
     features = 2 * len(FEATURES)
     return pl.pallas_call(
         lambda *refs: combine(rows, cols, *refs),

time: 19.7 us -> 18.8 us (0.954)
  blocking collectives: 15.4 us -> 14.5 us
    all_to_all x1, blocking collectives: 15.4 us -> 14.5 us  [on_device(): lax.all_to_all(sent.reshape(rows * cols, PIECE, 1, LANES), ('row', 'col')...]
where the time goes in v4:
time: 18.8 us; the launch traced here: 18.6 us
  blocking collectives  14.5 us (77%)
  Pallas kernels  3.66 us (19%)
  starting transfers between devices  0.45 us (2%)
    all_to_all x1, blocking collectives, on_device(): lax.all_to_all(sent.reshape(rows * cols, PIECE, 1, LANES), ('row', 'col')...  14.5 us
    pallas_call x1, Pallas kernels, on_device(): pl.pallas_call(lambda *refs: combine(rows, cols, *refs), out_shape=jax.Sh...  1.83 us
    pallas_call x1, Pallas kernels, on_device(): pl.pallas_call(lambda *refs: prepare(cols, *refs), out_shape=[pltpu.VMEM(...  1.49 us
    ppermute x1, starting transfers between devices, on_device(): other = lax.ppermute(image, 'row', [(i, i ^ 1) for i in range(rows)])  0.45 us
  transfers between devices with their start and end apart: 1, of which 0 were waited for; matrix products, arithmetic and copies ran while one was open for 0% of the time, Pallas kernels for 8%

profile of v4, /device:TPU:0, one launch (start us, length us, event | category | flops | bytes accessed | tf_op | source)
XLA Modules:
  0.0 18.6 jit_solution(10802389626496533234)
XLA Ops:
  0.0 0.5 %collective-permute-start = (f32[128,128]{1,0:T(8,128)}, f32[128,128]{1,0:T(8,128)S(1)}, u32[]{:S(2)}, u32[]{:S(2)}) collective-permute-start(f32[128,128]{1,0:T(8,128)} %refs_0_.1), channel_id=1, source_target_pairs={{0,4},{4,0},{8,12},{12,8},{16,20},{20,16},{24,28},{28,24},{1,5},{5... | collective-permute-start | bytes 196616 | tf_op jit(solution)/shard_map/ppermute | solution.py:479
  0.5 1.5 %prepare.1 = (f32[128,128]{1,0:T(8,128)S(1)}, bf16[2,2,3,128,256]{4,3,2,1,0:T(8,128)(2,1)S(1)}, bf16[2,256,768]{2,1,0:T(8,128)(2,1)S(1)}, bf16[2,48,128]{2,1,0:T...) custom-call(f32[128,128]{1,0:T(8,128)} %refs_0_.1, ...), custom_call_target="tpu_custom_call" | custom-call | flops 7864320 | bytes 4194304 | tf_op jit(solution)/shard_map/prepare/pallas_call | solution.py:480
  1.9 0.0 collective-permute-done.refs_0_
  2.0 0.3 %pack.1 = (f32[288,128]{1,0:T(8,128)S(1)}, f32[16,128]{1,0:T(8,128)S(1)}) custom-call(f32[128,128]{1,0:T(8,128)S(1)} %collective-permute-done.refs_0_, bf16[2,48,128]{2,1,0:T(8,128)(2,1)S(1)} %get-tuple-element.15.refs_1_, bf16[2,288,128]{2,1,0:T(8,128)(2,1)S(1)} %get-tuple-element.16.refs_2_, f32[48,128]{1,0:T(8,128)S(1)} %get-tuple-element.17.refs_3_, ...), custom_call_target="tpu_custom_call" | custom-call | tf_op jit(solution)/shard_map/pack/pallas_call | solution.py:505
  2.3 14.5 %all_to_all.5 = f32[32,9,1,128]{3,2,1,0:T(1,128)S(1)} all-to-all(f32[32,9,1,128]{3,2,1,0:T(1,128)S(1)} %bitcast.3), channel_id=1, replica_groups={{0,8,16,24,2,10,18,26,4,12,20,28,6,14,22,30,1,9,17,25,3,11,19,27,5,13,2..., dimensions={0} | all-to-all | bytes 294912 | tf_op jit(solution)/shard_map/all_to_all | solution.py:516
  16.8 1.8 %combine.1 = bf16[12,128,128]{2,1,0:T(8,128)(2,1)} custom-call(f32[128,128]{1,0:T(8,128)S(1)} %get-tuple-element.14.refs_0_, f32[288,128]{1,0:T(8,128)S(1)} %bitcast.2, f32[16,128]{1,0:T(8,128)S(1)} %get-tuple-element.20.refs_2_, bf16[2,2,3,128,256]{4,3,2,1,0:T(8,128)(2,1)S(1)} %get-tuple-element.21.refs_3_, bf16[2,256,768]{2,1,0:T(8,128)(2,1)S(1)} %get-tuple-element.22.refs_4_), custom_call_target="tpu_custom_call" | custom-call | tf_op jit(solution)/shard_map/combine/pallas_call | solution.py:524
Async XLA Ops:
  0.0 2.0 %collective-permute-start = (f32[128,128]{1,0:T(8,128)}, f32[128,128]{1,0:T(8,128)S(1)}, u32[]{:S(2)}, u32[]{:S(2)}) collective-permute-start(f32[128,128]{1,0:T(8,128)} %refs_0_.1), channel_id=1, source_target_pairs={{0,4},{4,0},{8,12},{12,8},{16,20},{20,16},{24,28},{28,24},{1,5},{5... | collective-permute-start | bytes 196616 | tf_op jit(solution)/shard_map/ppermute | solution.py:479

commit v5 on v4

--- a/solution.py
+++ b/solution.py
@@ -45,8 +45,8 @@
 BASIS = 24
 SENT = 16
 LANES = 128
-ROW_ROWS = 48
-COL_ROWS = 32
+OWN_ROWS, OTHER_ROWS, COL_ROWS = slice(0, 48), slice(48, 96), slice(96, 128)
+TILED_ROWS = slice(128, 128 + 2 * LANES)
 PIECE = SENT // 2 + 1
 
 
@@ -139,8 +139,7 @@
 
 
 def operator_tables(length, blocks, sources, gains):
-    remote = -(-SENT * len(sources(0)) // LANES) * LANES
-    tables = np.zeros((blocks, 2, 3, length, length + remote))
+    tables = np.zeros((blocks, 2, 3, length, length + SENT * len(sources(0))))
     total = length * blocks
     for block in range(blocks):
         cells = block * length + np.arange(length)
@@ -158,34 +157,6 @@
     return tables
 
 
-def window_tables(tables, length, blocks):
-    middle = blocks // 2
-    own = np.stack([tables[b, ..., :length] for b in (0, middle, blocks - 1)])
-    inner = np.zeros((2 * blocks - 1,) + tables.shape[1:-1] + (SENT,))
-    for block in range(blocks):
-        for source in range(1, blocks - 1):
-            start = length + SENT * source
-            inner[source - block + blocks - 1] = tables[block, ..., start : start + SENT]
-    ends = np.stack(
-        [
-            tables[..., length + SENT * end : length + SENT * (end + 1)]
-            for end in (0, blocks - 1)
-        ],
-        axis=1,
-    )
-
-    def cells_first(table, lead):
-        moved = np.moveaxis(table, -1, lead)
-        return moved.reshape(moved.shape[: lead + 1] + (-1,))
-
-    inner = cells_first(inner, 1)
-    return (
-        np.moveaxis(split_table(cells_first(own, 1)), 0, 1),
-        split_table(inner.reshape(-1, inner.shape[-1])),
-        np.moveaxis(split_table(cells_first(ends, 2)), 0, 2),
-    )
-
-
 def split_table(values):
     high = values.astype(ml_dtypes.bfloat16)
     low = (values - high.astype(np.float64)).astype(ml_dtypes.bfloat16)
@@ -207,61 +178,26 @@
 NT = ((1,), (1,))
 
 
-def prepare(
-    cols,
-    image,
-    row_sums,
-    col_sums,
-    row_op,
-    own_op,
-    inner_op,
-    ends_op,
-    block,
-    row_own,
-    col_own,
-    other_table,
-    col_table,
-    by_rows,
-    by_cols,
-    own_table,
-    sems,
-):
+def prepare(image, sums, row_op, col_op, col_rest, block, table, row_own, col_own, col_slots, by_rows, by_cols, sems):
     row, col = lax.axis_index("row"), lax.axis_index("col")
-    half = lax.rem(row, 2)
-    width = image.shape[1]
-    variant = jnp.where(col == 0, 0, jnp.where(col == cols - 1, 2, 1))
-    window = pl.multiple_of(SENT * (cols - col), SENT)
-    last = width + SENT * (cols - 1)
-
-    def col_rows(start, count):
-        return col_own.at[:, pl.ds(start, count)]
-
+    last = col_rest.shape[0] - 1
+    variant = jnp.where(col == 0, 0, jnp.where(col == last, 2, 1))
     pairs = [
         (image, block),
-        (row_sums.at[half], own_table),
-        (col_sums, col_table),
-        (row_sums.at[1 - half], other_table),
+        (sums.at[lax.rem(row, 2)], table),
         (row_op.at[row], row_own),
-        (own_op.at[variant], col_rows(0, width)),
-        (ends_op.at[col, 0], col_rows(width, SENT)),
-        (
-            inner_op.at[:, pl.ds(window, SENT * (cols - 2))],
-            col_rows(width + SENT, SENT * (cols - 2)),
-        ),
-        (ends_op.at[col, 1], col_rows(last, SENT)),
+        (col_op.at[variant], col_own),
+        (col_rest.at[col], col_slots),
     ]
     copies = [pltpu.make_async_copy(*pair, sems.at[i]) for i, pair in enumerate(pairs)]
     for copy in copies:
         copy.start()
-    for copy in copies[:3]:
+    for copy in copies[:2]:
         copy.wait()
     cells = split(block[...])
-    by_rows[...] = dot3([own_table[i] for i in range(2)], cells)
-    by_cols[...] = dot3([col_table[i, :COL_ROWS] for i in range(2)], cells, NT)
-    rest = col_own.shape[1] - last - SENT
-    if rest:
-        col_own[:, last + SENT :] = jnp.zeros((2, rest, col_own.shape[2]), jnp.bfloat16)
-    for copy in copies[3:]:
+    by_rows[...] = dot3([table[i, OWN_ROWS] for i in range(2)], cells)
+    by_cols[...] = dot3([table[i, COL_ROWS] for i in range(2)], cells, NT)
+    for copy in copies[2:]:
         copy.wait()
 
 
@@ -285,13 +221,13 @@
     return lax.broadcasted_iota(jnp.int32, shape, 1) // SENT
 
 
-def pack(rows, cols, other, other_table, col_table, by_rows, by_cols, sent, near):
+def pack(rows, cols, other, table, by_rows, by_cols, sent, near):
     row, col = lax.axis_index("row"), lax.axis_index("col")
     chip, half = row // 2, lax.rem(row, 2)
     cells = split(other[...])
     own_rows = by_rows[...]
-    other_rows = dot3([other_table[i] for i in range(2)], cells)
-    other_cols = dot3([col_table[i, :COL_ROWS] for i in range(2)], cells, NT)
+    other_rows = dot3([table[i, OTHER_ROWS] for i in range(2)], cells)
+    other_cols = dot3([table[i, COL_ROWS] for i in range(2)], cells, NT)
     near[...] = other_rows[BASIS : BASIS + SENT]
     over_rows = own_rows[:BASIS] + other_rows[:BASIS]
     own_near, other_near = own_rows[BASIS : BASIS + SENT], near[...]
@@ -307,7 +243,7 @@
     ]
     corners = dot3(
         split(jnp.concatenate([over_rows] + nears)),
-        [col_table[i, COL_ROWS:] for i in range(2)],
+        [table[i, TILED_ROWS] for i in range(2)],
         NT,
     )
 
@@ -320,14 +256,18 @@
         across.append([share(after(over_cols[to_half])), share(before(over_cols[to_half]))])
     for side in range(2):
         tiled = corners[:, LANES * side : LANES * (side + 1)]
-        mine = lane_place(tiled.shape) == lax.rem(col, LANES // SENT)
+        places = min(cols, LANES // SENT)
+        mine = lax.rem(lane_place(tiled.shape), places) == lax.rem(col, places)
         masked = jnp.where(mine, tiled, 0.0)
         placed.append([share(after(masked)), share(before(masked))])
         lines = []
         for to_half in range(2):
             start = BASIS + SENT * (1 - to_half)
             part = share(tiled[start : start + SENT])
-            diagonal = lane_place(part.shape) == lax.broadcasted_iota(jnp.int32, part.shape, 0)
+            line = lax.broadcasted_iota(jnp.int32, part.shape, 0)
+            diagonal = lax.rem(lane_place(part.shape) + line, LANES // SENT) == lax.rem(
+                col, LANES // SENT
+            )
             lines.append(jnp.sum(jnp.where(diagonal, part, 0.0), axis=0, keepdims=True))
         flat.append(lines)
     none = jnp.zeros((1, LANES), jnp.float32)
@@ -348,7 +288,22 @@
                 sent[at + PIECE - 1 : at + PIECE] = jnp.where(is_here, tail, none)
 
 
-def combine(rows, cols, block, got, near, row_own, col_own, out, staged, sems):
+def side_by_side(values, used):
+    high, low = split(values)
+    if used % LANES == 0:
+        return jnp.concatenate([high, low], axis=1)
+    lane = lax.broadcasted_iota(jnp.int32, values.shape, 1)
+    return jnp.where(lane < used, high, low)
+
+
+def long_product(own, beside, tall, rest):
+    left = jnp.concatenate([own[0], own[0], own[1], beside, beside], axis=1)
+    none = jnp.zeros(rest[1].shape, jnp.bfloat16)
+    right = jnp.concatenate([tall[0], tall[1], tall[0], rest[0], rest[0], rest[1], none])
+    return jnp.dot(left, right, preferred_element_type=jnp.float32)
+
+
+def combine(rows, cols, block, got, near, row_own, col_own, col_slots, out, staged, sems):
     row, col = lax.axis_index("row"), lax.axis_index("col")
     chip = row // 2
     length, width = block.shape
@@ -357,7 +312,6 @@
     order = exchange_order(rows, cols)
     nothing = jnp.zeros((SENT, LANES), jnp.float32)
     half_shape = (SENT // 2, LANES)
-    diagonal = lane_place(half_shape) == lax.broadcasted_iota(jnp.int32, half_shape, 0)
 
     def places(from_chip, from_col):
         devices = [(2 * from_chip + half) * cols + from_col for half in range(2)]
@@ -368,11 +322,10 @@
         return jnp.concatenate([got[at : at + PIECE - 1] for at in ats])
 
     def corner(from_chip, from_col):
-        ats = places(from_chip, from_col)
-        tails = [got[at + PIECE - 1 : at + PIECE] for at in ats]
-        return jnp.concatenate([jnp.where(diagonal, tail, 0.0) for tail in tails])
-
-    across, lower = [], []
+        tails = [got[at + PIECE - 1 : at + PIECE] for at in places(from_chip, from_col)]
+        return jnp.concatenate([jnp.broadcast_to(tail, half_shape) for tail in tails])
+
+    across = []
     corners = [nothing] * groups
     pieces = [[piece(i, j) for j in range(cols)] for i in range(rows // 2)]
     for from_col in range(cols):
@@ -382,15 +335,18 @@
             here = jnp.where(from_chip == chip, pieces[from_chip][from_col], here)
             tail = jnp.where(from_chip == chip, corner(from_chip, from_col), tail)
         across.append(here)
-        shift = LANES // 2
-        while shift >= SENT:
-            tail = tail + pltpu.roll(tail, shift, 1)
-            shift //= 2
+        tail = [
+            pltpu.roll(half, 0, 1, stride=SENT, stride_axis=0)
+            for half in (tail[: SENT // 2], tail[SENT // 2 :])
+        ]
+        tail = jnp.concatenate(tail)
         wanted = (lane_place(tail.shape) == from_col % per_group) & (from_col != col)
         corners[from_col // per_group] += jnp.where(wanted, tail, 0.0)
-    if groups * per_group > cols:
-        across.append(jnp.zeros((groups * LANES - SENT * cols, length), jnp.float32))
-    upper = jnp.concatenate([block[...], jnp.concatenate(across).T], axis=1)
+    if cols < per_group:
+        across = across * (per_group // cols)
+        corners = [part + pltpu.roll(part, SENT * cols, 1) for part in corners]
+    lines = [block[...]]
+    slots = [jnp.concatenate(across).T]
     for from_chip in range(rows // 2):
         is_here = from_chip == chip
         line = near[...]
@@ -401,24 +357,30 @@
             line = jnp.where(jnp.logical_not(is_here) & is_col, found, line)
             group = from_col // per_group
             parts[group] += jnp.where(is_here | is_col, 0.0, found)
-        lower.append(jnp.concatenate([line] + parts, axis=1))
-    known = split(jnp.concatenate([upper] + lower))
-    along_cols = dot3(known, [col_own[i] for i in range(2)])
-    fill = row_own.shape[-1] - along_cols.shape[0]
+        lines.append(line)
+        slots.append(jnp.concatenate(parts, axis=1))
+    along_cols = long_product(
+        split(jnp.concatenate(lines)),
+        side_by_side(jnp.concatenate(slots), SENT * cols),
+        [col_own[i] for i in range(2)],
+        [col_slots[i] for i in range(2)],
+    )
     copies = []
     for level in range(2):
         span = 3 * width
         smoothed = split(along_cols[:, span * level : span * (level + 1)])
-        if fill:
-            rest = jnp.zeros((fill, span), jnp.bfloat16)
-            smoothed = [jnp.concatenate([part, rest]) for part in smoothed]
-        products = [
-            dot3(
-                [row_own[i, level, k] for i in range(2)],
-                [part[:, : (3 - k) * width] for part in smoothed],
+        products = []
+        for k in range(3):
+            weights = row_own[level, k]
+            met = [part[:, : (3 - k) * width] for part in smoothed]
+            products.append(
+                long_product(
+                    [weights[:, :length], weights[:, length : 2 * length]],
+                    weights[:, 2 * length :],
+                    [part[:length] for part in met],
+                    [part[length:] for part in met],
+                )
             )
-            for k in range(3)
-        ]
         for f, (row_stencil, col_stencil) in enumerate(FEATURES):
             feature = products[row_stencil][:, width * col_stencil : width * (col_stencil + 1)]
             channel = len(FEATURES) * level + f
@@ -440,7 +402,7 @@
     base = [2.0 * math.sqrt(math.pi) * s for s in DEVIATIONS]
     gains = [[b * s**k for k in range(3)] for b, s in zip(base, DEVIATIONS)]
     whole, single = summary_table(2 * height), summary_table(height)
-    sums = np.zeros((2, ROW_ROWS, height))
+    sums = np.zeros((2, 48, height))
     for half, own in enumerate((after(single), before(single))):
         sums[half, :BASIS] = whole[:, half * height : (half + 1) * height]
         sums[half, BASIS : BASIS + SENT] = own
@@ -453,9 +415,9 @@
 
     gains = [[s**k for k in range(3)] for s in DEVIATIONS]
     single = summary_table(width)
-    sums = np.zeros((COL_ROWS + 2 * LANES, width))
+    sums = np.zeros((32 + 2 * LANES, width))
     sums[:BASIS] = single
-    sums[COL_ROWS:] = np.concatenate(
+    sums[32:] = np.concatenate(
         [np.tile(part, (LANES // SENT, 1)) for part in (after(single), before(single))]
     )
     return operator_tables(width, cols, sources, gains), sums
@@ -465,40 +427,41 @@
     height, width = image.shape
     row_weights, row_sums = row_tables(height, rows)
     col_weights, col_sums = col_tables(width, cols)
-    row_op = np.moveaxis(split_table(row_weights), 0, 1)
-    col_ops = window_tables(col_weights, width, cols)
-    row_sums = np.moveaxis(split_table(row_sums), 0, 1)
-    col_sums = split_table(col_sums)
+    high, low = split_table(row_weights)
+    row_op = np.concatenate(
+        [part[..., cells] for cells in (slice(height), slice(height, None)) for part in (high, low)],
+        axis=-1,
+    )
+    col_op = np.transpose(col_weights, (0, 4, 1, 2, 3))
+    col_op = np.moveaxis(split_table(col_op.reshape(*col_op.shape[:2], -1)), 0, 1)
+    col_rest = col_op[:, :, width:]
+    col_op = col_op[[0, cols // 2, cols - 1], :, :width]
+    sums = np.stack(
+        [np.concatenate([row_sums[h], row_sums[1 - h], col_sums]) for h in range(2)]
+    )
+    sums = np.moveaxis(split_table(sums), 0, 1)
 
     def in_vmem(count):
         return [pl.BlockSpec(memory_space=pltpu.VMEM)] * count
 
     params = pltpu.CompilerParams(vmem_limit_bytes=16 * 1024 * 1024)
-    operands = [jnp.asarray(x) for x in (row_sums, col_sums, row_op, *col_ops)]
+    operands = [jnp.asarray(x) for x in (sums, row_op, col_op, col_rest)]
     operands = [pltpu.with_memory_space_constraint(x, pltpu.HBM) for x in [image] + operands]
     other = lax.ppermute(image, "row", [(i, i ^ 1) for i in range(rows)])
-    block, row_own, col_own, other_table, col_table, by_rows, by_cols = pl.pallas_call(
-        lambda *refs: prepare(cols, *refs),
+    block, table, row_own, col_own, col_slots, by_rows, by_cols = pl.pallas_call(
+        prepare,
         out_shape=[
             pltpu.VMEM((height, width), jnp.float32),
-            pltpu.VMEM(row_op.shape[1:], jnp.bfloat16),
-            pltpu.VMEM((2, col_weights.shape[-1], 6 * width), jnp.bfloat16),
-            pltpu.VMEM(row_sums.shape[1:], jnp.bfloat16),
-            pltpu.VMEM(col_sums.shape, jnp.bfloat16),
-            pltpu.VMEM((ROW_ROWS, width), jnp.float32),
-            pltpu.VMEM((COL_ROWS, height), jnp.float32),
+            *[pltpu.VMEM(x.shape[1:], jnp.bfloat16) for x in (sums, row_op, col_op, col_rest)],
+            pltpu.VMEM((48, width), jnp.float32),
+            pltpu.VMEM((32, height), jnp.float32),
         ],
         in_specs=[pl.BlockSpec(memory_space=pltpu.HBM)] * len(operands),
         out_specs=in_vmem(7),
-        scratch_shapes=[
-            pltpu.VMEM(row_sums.shape[1:], jnp.bfloat16),
-            pltpu.SemaphoreType.DMA((9,)),
-        ],
+        scratch_shapes=[pltpu.SemaphoreType.DMA((5,))],
         compiler_params=params,
         cost_estimate=pl.CostEstimate(
-            flops=6 * (ROW_ROWS + COL_ROWS) * height * width,
-            bytes_accessed=4 * 1024 * 1024,
-            transcendentals=0,
+            flops=6 * 80 * height * width, bytes_accessed=4 * 1024 * 1024, transcendentals=0
         ),
         name="prepare",
     )(*operands)
@@ -508,11 +471,11 @@
             pltpu.VMEM((PIECE * rows * cols, LANES), jnp.float32),
             pltpu.VMEM((SENT, width), jnp.float32),
         ],
-        in_specs=in_vmem(5),
+        in_specs=in_vmem(4),
         out_specs=in_vmem(2),
         compiler_params=params,
         name="pack",
-    )(other, other_table, col_table, by_rows, by_cols)
+    )(other, table, by_rows, by_cols)
     got = lax.all_to_all(
         sent.reshape(rows * cols, PIECE, 1, LANES),
         ("row", "col"),
@@ -524,7 +487,7 @@
     return pl.pallas_call(
         lambda *refs: combine(rows, cols, *refs),
         out_shape=jax.ShapeDtypeStruct((features, height, width), jnp.bfloat16),
-        in_specs=in_vmem(5),
+        in_specs=in_vmem(6),
         out_specs=pl.BlockSpec(memory_space=pl.ANY),
         scratch_shapes=[
             pltpu.VMEM((features, height, width), jnp.bfloat16),
@@ -532,7 +495,7 @@
         ],
         compiler_params=params,
         name="combine",
-    )(block, got.reshape(sent.shape), near, row_own, col_own)
+    )(block, got.reshape(sent.shape), near, row_own, col_own, col_slots)
 
 
 def solution(mesh):

time: 18.8 us -> 18.6 us (0.989)
  Pallas kernels: 3.66 us -> 3.45 us
where the time goes in v5:
time: 18.6 us; the launch traced here: 18.4 us
  blocking collectives  14.5 us (78%)
  Pallas kernels  3.45 us (19%)
  starting transfers between devices  0.45 us (2%)
    all_to_all x1, blocking collectives, on_device(): lax.all_to_all(sent.reshape(rows * cols, PIECE, 1, LANES), ('row', 'col')...  14.5 us
    pallas_call x1, Pallas kernels, on_device(): pl.pallas_call(lambda *refs: combine(rows, cols, *refs), out_shape=jax.Sh...  1.71 us
    pallas_call x1, Pallas kernels, on_device(): pl.pallas_call(prepare, out_shape=[pltpu.VMEM((height, width), jnp.float3...  1.4 us
    ppermute x1, starting transfers between devices, on_device(): other = lax.ppermute(image, 'row', [(i, i ^ 1) for i in range(rows)])  0.45 us
  transfers between devices with their start and end apart: 1, of which 0 were waited for; matrix products, arithmetic and copies ran while one was open for 0% of the time, Pallas kernels for 8%

profile of v5, /device:TPU:0, one launch (start us, length us, event | category | flops | bytes accessed | tf_op | source)
XLA Modules:
  0.0 18.4 jit_solution(673632988930020600)
XLA Ops:
  0.0 0.5 %collective-permute-start = (f32[128,128]{1,0:T(8,128)}, f32[128,128]{1,0:T(8,128)S(1)}, u32[]{:S(2)}, u32[]{:S(2)}) collective-permute-start(f32[128,128]{1,0:T(8,128)} %image.1), channel_id=1, source_target_pairs={{0,4},{4,0},{8,12},{12,8},{16,20},{20,16},{24,28},{28,24},{1,5},{5... | collective-permute-start | bytes 196616 | tf_op jit(solution)/shard_map/ppermute | solution.py:450
  0.5 1.4 %prepare.1 = (f32[128,128]{1,0:T(8,128)S(1)}, bf16[2,384,128]{2,1,0:T(8,128)(2,1)S(1)}, bf16[2,3,128,384]{3,2,1,0:T(8,128)(2,1)S(1)}, bf16[2,128,768]{2,1,0:T(8,...) custom-call(f32[128,128]{1,0:T(8,128)} %image.1, ...), custom_call_target="tpu_custom_call" | custom-call | flops 7864320 | bytes 4194304 | tf_op jit(solution)/shard_map/prepare/pallas_call | solution.py:451
  1.9 0.0 collective-permute-done.refs_0_
  1.9 0.3 %pack.1 = (f32[288,128]{1,0:T(8,128)S(1)}, f32[16,128]{1,0:T(8,128)S(1)}) custom-call(f32[128,128]{1,0:T(8,128)S(1)} %collective-permute-done.refs_0_, bf16[2,384,128]{2,1,0:T(8,128)(2,1)S(1)} %get-tuple-element.15.refs_1_, f32[48,128]{1,0:T(8,128)S(1)} %get-tuple-element.16.refs_2_, f32[32,128]{1,0:T(8,128)S(1)} %get-tuple-element.17.refs_3_), custom_call_target="tpu_custom_call" | custom-call | tf_op jit(solution)/shard_map/pack/pallas_call | solution.py:468
  2.2 14.5 %all_to_all.5 = f32[32,9,1,128]{3,2,1,0:T(1,128)S(1)} all-to-all(f32[32,9,1,128]{3,2,1,0:T(1,128)S(1)} %bitcast.3), channel_id=1, replica_groups={{0,8,16,24,2,10,18,26,4,12,20,28,6,14,22,30,1,9,17,25,3,11,19,27,5,13,2..., dimensions={0} | all-to-all | bytes 294912 | tf_op jit(solution)/shard_map/all_to_all | solution.py:479
  16.7 1.7 %combine.1 = bf16[12,128,128]{2,1,0:T(8,128)(2,1)} custom-call(f32[128,128]{1,0:T(8,128)S(1)} %get-tuple-element.14.refs_0_, f32[288,128]{1,0:T(8,128)S(1)} %bitcast.2, f32[16,128]{1,0:T(8,128)S(1)} %get-tuple-element.19.refs_2_, bf16[2,3,128,384]{3,2,1,0:T(8,128)(2,1)S(1)} %get-tuple-element.20.refs_3_, bf16[2,128,768]{2,1,0:T(8,128)(2,1)S(1)} %get-tuple-element.21.refs_4_, ...), custom_call_target="tpu_custom_call" | custom-call | tf_op jit(solution)/shard_map/combine/pallas_call | solution.py:487
Async XLA Ops:
  0.0 1.9 %collective-permute-start = (f32[128,128]{1,0:T(8,128)}, f32[128,128]{1,0:T(8,128)S(1)}, u32[]{:S(2)}, u32[]{:S(2)}) collective-permute-start(f32[128,128]{1,0:T(8,128)} %image.1), channel_id=1, source_target_pairs={{0,4},{4,0},{8,12},{12,8},{16,20},{20,16},{24,28},{28,24},{1,5},{5... | collective-permute-start | bytes 196616 | tf_op jit(solution)/shard_map/ppermute | solution.py:450

commit v6 on v5

--- a/solution.py
+++ b/solution.py
@@ -46,7 +46,7 @@
 SENT = 16
 LANES = 128
 OWN_ROWS, OTHER_ROWS, COL_ROWS = slice(0, 48), slice(48, 96), slice(96, 128)
-TILED_ROWS = slice(128, 128 + 2 * LANES)
+TILED_ROWS = [slice(128, 144)] * (LANES // SENT) + [slice(144, 160)] * (LANES // SENT)
 PIECE = SENT // 2 + 1
 
 
@@ -178,27 +178,66 @@
 NT = ((1,), (1,))
 
 
-def prepare(image, sums, row_op, col_op, col_rest, block, table, row_own, col_own, col_slots, by_rows, by_cols, sems):
+def is_far(rows, cols):
     row, col = lax.axis_index("row"), lax.axis_index("col")
-    last = col_rest.shape[0] - 1
-    variant = jnp.where(col == 0, 0, jnp.where(col == last, 2, 1))
+    chip = row // 2
+    return col + chip // max(1, rows // 4) + lax.rem(chip, 2) >= 3
+
+
+def table_copies(cols, row_op, col_op, col_rest, row_own, col_own, col_slots, sems):
+    row, col = lax.axis_index("row"), lax.axis_index("col")
+    variant = jnp.where(col == 0, 0, jnp.where(col == cols - 1, 2, 1))
     pairs = [
-        (image, block),
-        (sums.at[lax.rem(row, 2)], table),
         (row_op.at[row], row_own),
         (col_op.at[variant], col_own),
         (col_rest.at[col], col_slots),
     ]
-    copies = [pltpu.make_async_copy(*pair, sems.at[i]) for i, pair in enumerate(pairs)]
+    return [pltpu.make_async_copy(*pair, sems.at[i]) for i, pair in enumerate(pairs)]
+
+
+def prepare(
+    rows,
+    cols,
+    image,
+    sums,
+    row_op,
+    col_op,
+    col_rest,
+    block,
+    table,
+    row_own,
+    col_own,
+    col_slots,
+    by_rows,
+    by_cols,
+    sems,
+    table_sems,
+):
+    half = lax.rem(lax.axis_index("row"), 2)
+    copies = [
+        pltpu.make_async_copy(image, block, sems.at[0]),
+        pltpu.make_async_copy(sums.at[half], table, sems.at[1]),
+    ]
+    tables = table_copies(cols, row_op, col_op, col_rest, row_own, col_own, col_slots, table_sems)
+    far = is_far(rows, cols)
     for copy in copies:
         copy.start()
-    for copy in copies[:2]:
+
+    @pl.when(jnp.logical_not(far))
+    def _():
+        for copy in tables:
+            copy.start()
+
+    for copy in copies:
         copy.wait()
     cells = split(block[...])
     by_rows[...] = dot3([table[i, OWN_ROWS] for i in range(2)], cells)
     by_cols[...] = dot3([table[i, COL_ROWS] for i in range(2)], cells, NT)
-    for copy in copies[2:]:
-        copy.wait()
+
+    @pl.when(jnp.logical_not(far))
+    def _():
+        for copy in tables:
+            copy.wait()
 
 
 def exchange_order(rows, cols):
@@ -243,7 +282,7 @@
     ]
     corners = dot3(
         split(jnp.concatenate([over_rows] + nears)),
-        [table[i, TILED_ROWS] for i in range(2)],
+        [jnp.concatenate([table[i, rows] for rows in TILED_ROWS]) for i in range(2)],
         NT,
     )
 
@@ -303,8 +342,38 @@
     return jnp.dot(left, right, preferred_element_type=jnp.float32)
 
 
-def combine(rows, cols, block, got, near, row_own, col_own, col_slots, out, staged, sems):
+def combine(
+    rows,
+    cols,
+    block,
+    got,
+    near,
+    row_op,
+    col_op,
+    col_rest,
+    row_loaded,
+    col_loaded,
+    slots_loaded,
+    out,
+    row_own,
+    col_own,
+    col_slots,
+    staged,
+    sems,
+    table_sems,
+):
     row, col = lax.axis_index("row"), lax.axis_index("col")
+
+    @pl.when(is_far(rows, cols))
+    def _():
+        tables = table_copies(
+            cols, row_op, col_op, col_rest, row_own, col_own, col_slots, table_sems
+        )
+        for copy in tables:
+            copy.start()
+        for copy in tables:
+            copy.wait()
+
     chip = row // 2
     length, width = block.shape
     groups = -(-SENT * cols // LANES)
@@ -415,11 +484,9 @@
 
     gains = [[s**k for k in range(3)] for s in DEVIATIONS]
     single = summary_table(width)
-    sums = np.zeros((32 + 2 * LANES, width))
+    sums = np.zeros((32 + 2 * SENT, width))
     sums[:BASIS] = single
-    sums[32:] = np.concatenate(
-        [np.tile(part, (LANES // SENT, 1)) for part in (after(single), before(single))]
-    )
+    sums[32:] = np.concatenate([after(single), before(single)])
     return operator_tables(width, cols, sources, gains), sums
 
 
@@ -449,7 +516,7 @@
     operands = [pltpu.with_memory_space_constraint(x, pltpu.HBM) for x in [image] + operands]
     other = lax.ppermute(image, "row", [(i, i ^ 1) for i in range(rows)])
     block, table, row_own, col_own, col_slots, by_rows, by_cols = pl.pallas_call(
-        prepare,
+        lambda *refs: prepare(rows, cols, *refs),
         out_shape=[
             pltpu.VMEM((height, width), jnp.float32),
             *[pltpu.VMEM(x.shape[1:], jnp.bfloat16) for x in (sums, row_op, col_op, col_rest)],
@@ -458,7 +525,7 @@
         ],
         in_specs=[pl.BlockSpec(memory_space=pltpu.HBM)] * len(operands),
         out_specs=in_vmem(7),
-        scratch_shapes=[pltpu.SemaphoreType.DMA((5,))],
+        scratch_shapes=[pltpu.SemaphoreType.DMA((2,)), pltpu.SemaphoreType.DMA((3,))],
         compiler_params=params,
         cost_estimate=pl.CostEstimate(
             flops=6 * 80 * height * width, bytes_accessed=4 * 1024 * 1024, transcendentals=0
@@ -484,18 +551,25 @@
         axis_index_groups=[exchange_order(rows, cols)],
     )
     features = 2 * len(FEATURES)
-    return pl.pallas_call(
+    weights = [row_own, col_own, col_slots]
+    result = pl.pallas_call(
         lambda *refs: combine(rows, cols, *refs),
-        out_shape=jax.ShapeDtypeStruct((features, height, width), jnp.bfloat16),
-        in_specs=in_vmem(6),
-        out_specs=pl.BlockSpec(memory_space=pl.ANY),
+        out_shape=[
+            jax.ShapeDtypeStruct((features, height, width), jnp.bfloat16),
+            *[pltpu.VMEM(x.shape, x.dtype) for x in weights],
+        ],
+        in_specs=in_vmem(3) + [pl.BlockSpec(memory_space=pltpu.HBM)] * 3 + in_vmem(3),
+        out_specs=[pl.BlockSpec(memory_space=pl.ANY)] + in_vmem(3),
+        input_output_aliases={6: 1, 7: 2, 8: 3},
         scratch_shapes=[
             pltpu.VMEM((features, height, width), jnp.bfloat16),
             pltpu.SemaphoreType.DMA((features,)),
+            pltpu.SemaphoreType.DMA((3,)),
         ],
         compiler_params=params,
         name="combine",
-    )(block, got.reshape(sent.shape), near, row_own, col_own, col_slots)
+    )(block, got.reshape(sent.shape), near, *operands[2:], *weights)
+    return result[0]
 
 
 def solution(mesh):

time: 18.6 us -> 18.5 us (level)
  transfers between devices with their start and end apart: 1 -> 1, of which waited for: 0 -> 0; matrix products, arithmetic and copies ran while one was open for 0% -> 0% of each run, Pallas kernels for 8% -> 7%
where the time goes in v6:
time: 18.5 us; the launch traced here: 18.4 us
  blocking collectives  14.5 us (78%)
  Pallas kernels  3.39 us (18%)
  starting transfers between devices  0.45 us (2%)
    all_to_all x1, blocking collectives, on_device(): lax.all_to_all(sent.reshape(rows * cols, PIECE, 1, LANES), ('row', 'col')...  14.5 us
    pallas_call x1, Pallas kernels, on_device(): pl.pallas_call(lambda *refs: combine(rows, cols, *refs), out_shape=[jax.S...  1.71 us
    pallas_call x1, Pallas kernels, on_device(): pl.pallas_call(lambda *refs: prepare(rows, cols, *refs), out_shape=[pltpu...  1.34 us
    ppermute x1, starting transfers between devices, on_device(): other = lax.ppermute(image, 'row', [(i, i ^ 1) for i in range(rows)])  0.45 us
  transfers between devices with their start and end apart: 1, of which 0 were waited for; matrix products, arithmetic and copies ran while one was open for 0% of the time, Pallas kernels for 7%

profile of v6, /device:TPU:0, one launch (start us, length us, event | category | flops | bytes accessed | tf_op | source)
XLA Modules:
  0.0 18.4 jit_solution(10980920314034315842)
XLA Ops:
  0.0 0.5 %collective-permute-start = (f32[128,128]{1,0:T(8,128)}, f32[128,128]{1,0:T(8,128)S(1)}, u32[]{:S(2)}, u32[]{:S(2)}) collective-permute-start(f32[128,128]{1,0:T(8,128)} %refs_0_.1), channel_id=1, source_target_pairs={{0,4},{4,0},{8,12},{12,8},{16,20},{20,16},{24,28},{28,24},{1,5},{5... | collective-permute-start | bytes 196616 | tf_op jit(solution)/shard_map/ppermute | solution.py:517
  0.5 1.3 %prepare.1 = (f32[128,128]{1,0:T(8,128)S(1)}, bf16[2,160,128]{2,1,0:T(8,128)(2,1)S(1)}, bf16[2,3,128,384]{3,2,1,0:T(8,128)(2,1)S(1)}, bf16[2,128,768]{2,1,0:T(8,...) custom-call(f32[128,128]{1,0:T(8,128)} %refs_0_.1, ...), custom_call_target="tpu_custom_call" | custom-call | flops 7864320 | bytes 4194304 | tf_op jit(solution)/shard_map/prepare/pallas_call | solution.py:518
  1.8 0.0 collective-permute-done.refs_0_
  1.8 0.3 %pack.1 = (f32[288,128]{1,0:T(8,128)S(1)}, f32[16,128]{1,0:T(8,128)S(1)}) custom-call(f32[128,128]{1,0:T(8,128)S(1)} %collective-permute-done.refs_0_, bf16[2,160,128]{2,1,0:T(8,128)(2,1)S(1)} %get-tuple-element.16.refs_1_, f32[48,128]{1,0:T(8,128)S(1)} %get-tuple-element.17.refs_2_, f32[32,128]{1,0:T(8,128)S(1)} %get-tuple-element.18.refs_3_), custom_call_target="tpu_custom_call" | custom-call | tf_op jit(solution)/shard_map/pack/pallas_call | solution.py:535
  2.2 14.5 %all_to_all.5 = f32[32,9,1,128]{3,2,1,0:T(1,128)S(1)} all-to-all(f32[32,9,1,128]{3,2,1,0:T(1,128)S(1)} %bitcast.3), channel_id=1, replica_groups={{0,8,16,24,2,10,18,26,4,12,20,28,6,14,22,30,1,9,17,25,3,11,19,27,5,13,2..., dimensions={0} | all-to-all | bytes 294912 | tf_op jit(solution)/shard_map/all_to_all | solution.py:546
  16.7 1.7 %combine.1 = (bf16[12,128,128]{2,1,0:T(8,128)(2,1)}, bf16[2,3,128,384]{3,2,1,0:T(8,128)(2,1)S(1)}, bf16[2,128,768]{2,1,0:T(8,128)(2,1)S(1)}, bf16[2,64,768]{2,1,0:T(8,128)(2,1)S(1)}) custom-call(f32[128,128]{1,0:T(8,128)S(1)} %get-tuple-element.15.refs_0_, f32[288,128]{1,0:T(8,128)S(1)} %bitcast.2, ...), custom_call_target="tpu_custom_call", output_to_operand_aliasing={{1}: (6, {}), {2}: (7, {}), {3}: (8, {})} | custom-call | tf_op jit(solution)/shard_map/combine/pallas_call | solution.py:555
Async XLA Ops:
  0.0 1.8 %collective-permute-start = (f32[128,128]{1,0:T(8,128)}, f32[128,128]{1,0:T(8,128)S(1)}, u32[]{:S(2)}, u32[]{:S(2)}) collective-permute-start(f32[128,128]{1,0:T(8,128)} %refs_0_.1), channel_id=1, source_target_pairs={{0,4},{4,0},{8,12},{12,8},{16,20},{20,16},{24,28},{28,24},{1,5},{5... | collective-permute-start | bytes 196616 | tf_op jit(solution)/shard_map/ppermute | solution.py:517

commit v7 on v6

--- a/solution.py
+++ b/solution.py
@@ -243,7 +243,8 @@
 def exchange_order(rows, cols):
     def place(device):
         row, col = divmod(device, cols)
-        return col % 2, row % 2, col // 2, row // 2
+        chip, half = divmod(row, 2)
+        return (col ^ half) % 2, (col ^ chip ^ chip // 2) % 2, col // 2, chip
 
     return sorted(range(rows * cols), key=place)
 

time: 18.5 us -> 18.4 us (level)
  no operation moved by 1% of the time
where the time goes in v7:
time: 18.4 us; the launch traced here: 18.2 us
  blocking collectives  14.4 us (78%)
  Pallas kernels  3.39 us (18%)
  starting transfers between devices  0.45 us (2%)
    all_to_all x1, blocking collectives, on_device(): lax.all_to_all(sent.reshape(rows * cols, PIECE, 1, LANES), ('row', 'col')...  14.4 us
    pallas_call x1, Pallas kernels, on_device(): pl.pallas_call(lambda *refs: combine(rows, cols, *refs), out_shape=[jax.S...  1.71 us
    pallas_call x1, Pallas kernels, on_device(): pl.pallas_call(lambda *refs: prepare(rows, cols, *refs), out_shape=[pltpu...  1.34 us
    ppermute x1, starting transfers between devices, on_device(): other = lax.ppermute(image, 'row', [(i, i ^ 1) for i in range(rows)])  0.45 us
  transfers between devices with their start and end apart: 1, of which 0 were waited for; matrix products, arithmetic and copies ran while one was open for 0% of the time, Pallas kernels for 7%

profile of v7, /device:TPU:0, one launch (start us, length us, event | category | flops | bytes accessed | tf_op | source)
XLA Modules:
  0.0 18.2 jit_solution(7679335124897780592)
XLA Ops:
  0.0 0.5 %collective-permute-start = (f32[128,128]{1,0:T(8,128)}, f32[128,128]{1,0:T(8,128)S(1)}, u32[]{:S(2)}, u32[]{:S(2)}) collective-permute-start(f32[128,128]{1,0:T(8,128)} %refs_0_.1), channel_id=1, source_target_pairs={{0,4},{4,0},{8,12},{12,8},{16,20},{20,16},{24,28},{28,24},{1,5},{5... | collective-permute-start | bytes 196616 | tf_op jit(solution)/shard_map/ppermute | solution.py:518
  0.5 1.3 %prepare.1 = (f32[128,128]{1,0:T(8,128)S(1)}, bf16[2,160,128]{2,1,0:T(8,128)(2,1)S(1)}, bf16[2,3,128,384]{3,2,1,0:T(8,128)(2,1)S(1)}, bf16[2,128,768]{2,1,0:T(8,...) custom-call(f32[128,128]{1,0:T(8,128)} %refs_0_.1, ...), custom_call_target="tpu_custom_call" | custom-call | flops 7864320 | bytes 4194304 | tf_op jit(solution)/shard_map/prepare/pallas_call | solution.py:519
  1.8 0.0 collective-permute-done.refs_0_
  1.8 0.3 %pack.1 = (f32[288,128]{1,0:T(8,128)S(1)}, f32[16,128]{1,0:T(8,128)S(1)}) custom-call(f32[128,128]{1,0:T(8,128)S(1)} %collective-permute-done.refs_0_, bf16[2,160,128]{2,1,0:T(8,128)(2,1)S(1)} %get-tuple-element.16.refs_1_, f32[48,128]{1,0:T(8,128)S(1)} %get-tuple-element.17.refs_2_, f32[32,128]{1,0:T(8,128)S(1)} %get-tuple-element.18.refs_3_), custom_call_target="tpu_custom_call" | custom-call | tf_op jit(solution)/shard_map/pack/pallas_call | solution.py:536
  2.2 14.4 %all_to_all.5 = f32[32,9,1,128]{3,2,1,0:T(1,128)S(1)} all-to-all(f32[32,9,1,128]{3,2,1,0:T(1,128)S(1)} %bitcast.3), channel_id=1, replica_groups={{0,13,21,24,2,15,23,26,5,8,16,29,7,10,18,31,4,9,17,28,6,11,19,30,1,12,2..., dimensions={0} | all-to-all | bytes 294912 | tf_op jit(solution)/shard_map/all_to_all | solution.py:547
  16.5 1.7 %combine.1 = (bf16[12,128,128]{2,1,0:T(8,128)(2,1)}, bf16[2,3,128,384]{3,2,1,0:T(8,128)(2,1)S(1)}, bf16[2,128,768]{2,1,0:T(8,128)(2,1)S(1)}, bf16[2,64,768]{2,1,0:T(8,128)(2,1)S(1)}) custom-call(f32[128,128]{1,0:T(8,128)S(1)} %get-tuple-element.15.refs_0_, f32[288,128]{1,0:T(8,128)S(1)} %bitcast.2, ...), custom_call_target="tpu_custom_call", output_to_operand_aliasing={{1}: (6, {}), {2}: (7, {}), {3}: (8, {})} | custom-call | tf_op jit(solution)/shard_map/combine/pallas_call | solution.py:556
Async XLA Ops:
  0.0 1.8 %collective-permute-start = (f32[128,128]{1,0:T(8,128)}, f32[128,128]{1,0:T(8,128)S(1)}, u32[]{:S(2)}, u32[]{:S(2)}) collective-permute-start(f32[128,128]{1,0:T(8,128)} %refs_0_.1), channel_id=1, source_target_pairs={{0,4},{4,0},{8,12},{12,8},{16,20},{20,16},{24,28},{28,24},{1,5},{5... | collective-permute-start | bytes 196616 | tf_op jit(solution)/shard_map/ppermute | solution.py:518

commit v8 on v7

--- a/solution.py
+++ b/solution.py
@@ -195,6 +195,28 @@
     return [pltpu.make_async_copy(*pair, sems.at[i]) for i, pair in enumerate(pairs)]
 
 
+def side_by_side(values, used):
+    high, low = split(values)
+    if used % LANES == 0:
+        return jnp.concatenate([high, low], axis=1)
+    lane = lax.broadcasted_iota(jnp.int32, values.shape, 1)
+    return jnp.where(lane < used, high, low)
+
+
+def long_product(own, beside, tall, rest):
+    left = jnp.concatenate([own[0], own[0], own[1], beside, beside], axis=1)
+    none = jnp.zeros(rest[1].shape, jnp.bfloat16)
+    right = jnp.concatenate([tall[0], tall[1], tall[0], rest[0], rest[0], rest[1], none])
+    return jnp.dot(left, right, preferred_element_type=jnp.float32)
+
+
+def short_product(beside, rest):
+    none = jnp.zeros(rest[1].shape, jnp.bfloat16)
+    left = jnp.concatenate([beside, beside], axis=1)
+    right = jnp.concatenate([rest[0], rest[0], rest[1], none])
+    return jnp.dot(left, right, preferred_element_type=jnp.float32)
+
+
 def prepare(
     rows,
     cols,
@@ -210,6 +232,7 @@
     col_slots,
     by_rows,
     by_cols,
+    ahead,
     sems,
     table_sems,
 ):
@@ -238,6 +261,7 @@
     def _():
         for copy in tables:
             copy.wait()
+        ahead[...] = dot3(split(block[...]), [col_own[i] for i in range(2)])
 
 
 def exchange_order(rows, cols):
@@ -328,21 +352,6 @@
                 sent[at + PIECE - 1 : at + PIECE] = jnp.where(is_here, tail, none)
 
 
-def side_by_side(values, used):
-    high, low = split(values)
-    if used % LANES == 0:
-        return jnp.concatenate([high, low], axis=1)
-    lane = lax.broadcasted_iota(jnp.int32, values.shape, 1)
-    return jnp.where(lane < used, high, low)
-
-
-def long_product(own, beside, tall, rest):
-    left = jnp.concatenate([own[0], own[0], own[1], beside, beside], axis=1)
-    none = jnp.zeros(rest[1].shape, jnp.bfloat16)
-    right = jnp.concatenate([tall[0], tall[1], tall[0], rest[0], rest[0], rest[1], none])
-    return jnp.dot(left, right, preferred_element_type=jnp.float32)
-
-
 def combine(
     rows,
     cols,
@@ -355,10 +364,12 @@
     row_loaded,
     col_loaded,
     slots_loaded,
+    ahead_known,
     out,
     row_own,
     col_own,
     col_slots,
+    ahead,
     staged,
     sems,
     table_sems,
@@ -374,6 +385,7 @@
             copy.start()
         for copy in tables:
             copy.wait()
+        ahead[...] = dot3(split(block[...]), [col_own[i] for i in range(2)])
 
     chip = row // 2
     length, width = block.shape
@@ -415,8 +427,8 @@
     if cols < per_group:
         across = across * (per_group // cols)
         corners = [part + pltpu.roll(part, SENT * cols, 1) for part in corners]
-    lines = [block[...]]
-    slots = [jnp.concatenate(across).T]
+    lines, slots = [], []
+    own_slots = jnp.concatenate(across).T
     for from_chip in range(rows // 2):
         is_here = from_chip == chip
         line = near[...]
@@ -429,11 +441,17 @@
             parts[group] += jnp.where(is_here | is_col, 0.0, found)
         lines.append(line)
         slots.append(jnp.concatenate(parts, axis=1))
-    along_cols = long_product(
-        split(jnp.concatenate(lines)),
-        side_by_side(jnp.concatenate(slots), SENT * cols),
-        [col_own[i] for i in range(2)],
-        [col_slots[i] for i in range(2)],
+    rest = [col_slots[i] for i in range(2)]
+    along_cols = jnp.concatenate(
+        [
+            ahead[...] + short_product(side_by_side(own_slots, SENT * cols), rest),
+            long_product(
+                split(jnp.concatenate(lines)),
+                side_by_side(jnp.concatenate(slots), SENT * cols),
+                [col_own[i] for i in range(2)],
+                rest,
+            ),
+        ]
     )
     copies = []
     for level in range(2):
@@ -516,16 +534,17 @@
     operands = [jnp.asarray(x) for x in (sums, row_op, col_op, col_rest)]
     operands = [pltpu.with_memory_space_constraint(x, pltpu.HBM) for x in [image] + operands]
     other = lax.ppermute(image, "row", [(i, i ^ 1) for i in range(rows)])
-    block, table, row_own, col_own, col_slots, by_rows, by_cols = pl.pallas_call(
+    block, table, row_own, col_own, col_slots, by_rows, by_cols, ahead = pl.pallas_call(
         lambda *refs: prepare(rows, cols, *refs),
         out_shape=[
             pltpu.VMEM((height, width), jnp.float32),
             *[pltpu.VMEM(x.shape[1:], jnp.bfloat16) for x in (sums, row_op, col_op, col_rest)],
             pltpu.VMEM((48, width), jnp.float32),
             pltpu.VMEM((32, height), jnp.float32),
+            pltpu.VMEM((height, 6 * width), jnp.float32),
         ],
         in_specs=[pl.BlockSpec(memory_space=pltpu.HBM)] * len(operands),
-        out_specs=in_vmem(7),
+        out_specs=in_vmem(8),
         scratch_shapes=[pltpu.SemaphoreType.DMA((2,)), pltpu.SemaphoreType.DMA((3,))],
         compiler_params=params,
         cost_estimate=pl.CostEstimate(
@@ -552,16 +571,16 @@
         axis_index_groups=[exchange_order(rows, cols)],
     )
     features = 2 * len(FEATURES)
-    weights = [row_own, col_own, col_slots]
+    kept = [row_own, col_own, col_slots, ahead]
     result = pl.pallas_call(
         lambda *refs: combine(rows, cols, *refs),
         out_shape=[
             jax.ShapeDtypeStruct((features, height, width), jnp.bfloat16),
-            *[pltpu.VMEM(x.shape, x.dtype) for x in weights],
+            *[pltpu.VMEM(x.shape, x.dtype) for x in kept],
         ],
-        in_specs=in_vmem(3) + [pl.BlockSpec(memory_space=pltpu.HBM)] * 3 + in_vmem(3),
-        out_specs=[pl.BlockSpec(memory_space=pl.ANY)] + in_vmem(3),
-        input_output_aliases={6: 1, 7: 2, 8: 3},
+        in_specs=in_vmem(3) + [pl.BlockSpec(memory_space=pltpu.HBM)] * 3 + in_vmem(4),
+        out_specs=[pl.BlockSpec(memory_space=pl.ANY)] + in_vmem(4),
+        input_output_aliases={6: 1, 7: 2, 8: 3, 9: 4},
         scratch_shapes=[
             pltpu.VMEM((features, height, width), jnp.bfloat16),
             pltpu.SemaphoreType.DMA((features,)),
@@ -569,7 +588,7 @@
         ],
         compiler_params=params,
         name="combine",
-    )(block, got.reshape(sent.shape), near, *operands[2:], *weights)
+    )(block, got.reshape(sent.shape), near, *operands[2:], *kept)
     return result[0]
 
 

time: 18.4 us -> 18.4 us (level)
  blocking collectives: 14.4 us -> 14.1 us
  Pallas kernels: 3.39 us -> 3.61 us
    pallas_call x1, Pallas kernels: 1.34 us -> 1.61 us  [on_device(): pl.pallas_call(lambda *refs: prepare(rows, cols, *refs), out_shape=[pltpu...]
    all_to_all x1, blocking collectives: 14.4 us -> 14.1 us  [on_device(): lax.all_to_all(sent.reshape(rows * cols, PIECE, 1, LANES), ('row', 'col')...]
  transfers between devices with their start and end apart: 1 -> 1, of which waited for: 0 -> 0; matrix products, arithmetic and copies ran while one was open for 0% -> 0% of each run, Pallas kernels for 7% -> 9%
where the time goes in v8:
time: 18.4 us; the launch traced here: 18.2 us
  blocking collectives  14.1 us (77%)
  Pallas kernels  3.61 us (20%)
  starting transfers between devices  0.45 us (2%)
    all_to_all x1, blocking collectives, on_device(): lax.all_to_all(sent.reshape(rows * cols, PIECE, 1, LANES), ('row', 'col')...  14.1 us
    pallas_call x1, Pallas kernels, on_device(): pl.pallas_call(lambda *refs: combine(rows, cols, *refs), out_shape=[jax.S...  1.66 us
    pallas_call x1, Pallas kernels, on_device(): pl.pallas_call(lambda *refs: prepare(rows, cols, *refs), out_shape=[pltpu...  1.61 us
    ppermute x1, starting transfers between devices, on_device(): other = lax.ppermute(image, 'row', [(i, i ^ 1) for i in range(rows)])  0.45 us
  transfers between devices with their start and end apart: 1, of which 0 were waited for; matrix products, arithmetic and copies ran while one was open for 0% of the time, Pallas kernels for 9%

profile of v8, /device:TPU:0, one launch (start us, length us, event | category | flops | bytes accessed | tf_op | source)
XLA Modules:
  0.0 18.2 jit_solution(12865513484493227809)
XLA Ops:
  0.0 0.5 %collective-permute-start = (f32[128,128]{1,0:T(8,128)}, f32[128,128]{1,0:T(8,128)S(1)}, u32[]{:S(2)}, u32[]{:S(2)}) collective-permute-start(f32[128,128]{1,0:T(8,128)} %refs_0_.1), channel_id=1, source_target_pairs={{0,4},{4,0},{8,12},{12,8},{16,20},{20,16},{24,28},{28,24},{1,5},{5... | collective-permute-start | bytes 196616 | tf_op jit(solution)/shard_map/ppermute | solution.py:536
  0.5 1.6 %prepare.1 = (f32[128,128]{1,0:T(8,128)S(1)}, bf16[2,160,128]{2,1,0:T(8,128)(2,1)S(1)}, bf16[2,3,128,384]{3,2,1,0:T(8,128)(2,1)S(1)}, bf16[2,128,768]{2,1,0:T(8,...) custom-call(f32[128,128]{1,0:T(8,128)} %refs_0_.1, ...), custom_call_target="tpu_custom_call" | custom-call | flops 7864320 | bytes 4194304 | tf_op jit(solution)/shard_map/prepare/pallas_call | solution.py:537
  2.1 0.0 collective-permute-done.refs_0_
  2.1 0.3 %pack.1 = (f32[288,128]{1,0:T(8,128)S(1)}, f32[16,128]{1,0:T(8,128)S(1)}) custom-call(f32[128,128]{1,0:T(8,128)S(1)} %collective-permute-done.refs_0_, bf16[2,160,128]{2,1,0:T(8,128)(2,1)S(1)} %get-tuple-element.17.refs_1_, f32[48,128]{1,0:T(8,128)S(1)} %get-tuple-element.18.refs_2_, f32[32,128]{1,0:T(8,128)S(1)} %get-tuple-element.19.refs_3_), custom_call_target="tpu_custom_call" | custom-call | tf_op jit(solution)/shard_map/pack/pallas_call | solution.py:555
  2.4 14.1 %all_to_all.5 = f32[32,9,1,128]{3,2,1,0:T(1,128)S(1)} all-to-all(f32[32,9,1,128]{3,2,1,0:T(1,128)S(1)} %bitcast.3), channel_id=1, replica_groups={{0,13,21,24,2,15,23,26,5,8,16,29,7,10,18,31,4,9,17,28,6,11,19,30,1,12,2..., dimensions={0} | all-to-all | bytes 294912 | tf_op jit(solution)/shard_map/all_to_all | solution.py:566
  16.5 1.7 %combine.1 = (bf16[12,128,128]{2,1,0:T(8,128)(2,1)}, bf16[2,3,128,384]{3,2,1,0:T(8,128)(2,1)S(1)}, bf16[2,128,768]{2,1,0:T(8,128)(2,1)S(1)}, bf16[2,64,768]{2,1,0:T(8,128)(2,1)S(1)}, f32[128,768]{1,0:T(8,128)S(1)}) custom-call(f32[128,128]{1,0:T(8,128)S(1)} %get-tuple-element.16.refs_0_, ...), custom_call_target="tpu_custom_call", output_to_operand_aliasing={{1}: (6, {}), {2}: (7, {}), {3}: (8, {}), {4}: (9, {})} | custom-call | tf_op jit(solution)/shard_map/combine/pallas_call | solution.py:575
Async XLA Ops:
  0.0 2.1 %collective-permute-start = (f32[128,128]{1,0:T(8,128)}, f32[128,128]{1,0:T(8,128)S(1)}, u32[]{:S(2)}, u32[]{:S(2)}) collective-permute-start(f32[128,128]{1,0:T(8,128)} %refs_0_.1), channel_id=1, source_target_pairs={{0,4},{4,0},{8,12},{12,8},{16,20},{20,16},{24,28},{28,24},{1,5},{5... | collective-permute-start | bytes 196616 | tf_op jit(solution)/shard_map/ppermute | solution.py:536

commit v9 on v8

--- a/solution.py
+++ b/solution.py
@@ -268,7 +268,7 @@
     def place(device):
         row, col = divmod(device, cols)
         chip, half = divmod(row, 2)
-        return (col ^ half) % 2, (col ^ chip ^ chip // 2) % 2, col // 2, chip
+        return -((col ^ half) % 2), (col ^ chip ^ chip // 2) % 2, col // 2, chip
 
     return sorted(range(rows * cols), key=place)
 

time: 18.4 us -> 18.4 us (level)
  no operation moved by 1% of the time
where the time goes in v9:
time: 18.4 us; the launch traced here: 18.2 us
  blocking collectives  14.1 us (77%)
  Pallas kernels  3.61 us (20%)
  starting transfers between devices  0.45 us (2%)
    all_to_all x1, blocking collectives, on_device(): lax.all_to_all(sent.reshape(rows * cols, PIECE, 1, LANES), ('row', 'col')...  14.1 us
    pallas_call x1, Pallas kernels, on_device(): pl.pallas_call(lambda *refs: combine(rows, cols, *refs), out_shape=[jax.S...  1.67 us
    pallas_call x1, Pallas kernels, on_device(): pl.pallas_call(lambda *refs: prepare(rows, cols, *refs), out_shape=[pltpu...  1.61 us
    ppermute x1, starting transfers between devices, on_device(): other = lax.ppermute(image, 'row', [(i, i ^ 1) for i in range(rows)])  0.45 us
  transfers between devices with their start and end apart: 1, of which 0 were waited for; matrix products, arithmetic and copies ran while one was open for 0% of the time, Pallas kernels for 9%

profile of v9, /device:TPU:0, one launch (start us, length us, event | category | flops | bytes accessed | tf_op | source)
XLA Modules:
  0.0 18.2 jit_solution(5986855080854162576)
XLA Ops:
  0.0 0.5 %collective-permute-start = (f32[128,128]{1,0:T(8,128)}, f32[128,128]{1,0:T(8,128)S(1)}, u32[]{:S(2)}, u32[]{:S(2)}) collective-permute-start(f32[128,128]{1,0:T(8,128)} %refs_0_.1), channel_id=1, source_target_pairs={{0,4},{4,0},{8,12},{12,8},{16,20},{20,16},{24,28},{28,24},{1,5},{5... | collective-permute-start | bytes 196616 | tf_op jit(solution)/shard_map/ppermute | solution.py:536
  0.5 1.6 %prepare.1 = (f32[128,128]{1,0:T(8,128)S(1)}, bf16[2,160,128]{2,1,0:T(8,128)(2,1)S(1)}, bf16[2,3,128,384]{3,2,1,0:T(8,128)(2,1)S(1)}, bf16[2,128,768]{2,1,0:T(8,...) custom-call(f32[128,128]{1,0:T(8,128)} %refs_0_.1, ...), custom_call_target="tpu_custom_call" | custom-call | flops 7864320 | bytes 4194304 | tf_op jit(solution)/shard_map/prepare/pallas_call | solution.py:537
  2.1 0.0 collective-permute-done.refs_0_
  2.1 0.3 %pack.1 = (f32[288,128]{1,0:T(8,128)S(1)}, f32[16,128]{1,0:T(8,128)S(1)}) custom-call(f32[128,128]{1,0:T(8,128)S(1)} %collective-permute-done.refs_0_, bf16[2,160,128]{2,1,0:T(8,128)(2,1)S(1)} %get-tuple-element.17.refs_1_, f32[48,128]{1,0:T(8,128)S(1)} %get-tuple-element.18.refs_2_, f32[32,128]{1,0:T(8,128)S(1)} %get-tuple-element.19.refs_3_), custom_call_target="tpu_custom_call" | custom-call | tf_op jit(solution)/shard_map/pack/pallas_call | solution.py:555
  2.4 14.1 %all_to_all.5 = f32[32,9,1,128]{3,2,1,0:T(1,128)S(1)} all-to-all(f32[32,9,1,128]{3,2,1,0:T(1,128)S(1)} %bitcast.3), channel_id=1, replica_groups={{4,9,17,28,6,11,19,30,1,12,20,25,3,14,22,27,0,13,21,24,2,15,23,26,5,8,1..., dimensions={0} | all-to-all | bytes 294912 | tf_op jit(solution)/shard_map/all_to_all | solution.py:566
  16.5 1.7 %combine.1 = (bf16[12,128,128]{2,1,0:T(8,128)(2,1)}, bf16[2,3,128,384]{3,2,1,0:T(8,128)(2,1)S(1)}, bf16[2,128,768]{2,1,0:T(8,128)(2,1)S(1)}, bf16[2,64,768]{2,1,0:T(8,128)(2,1)S(1)}, f32[128,768]{1,0:T(8,128)S(1)}) custom-call(f32[128,128]{1,0:T(8,128)S(1)} %get-tuple-element.16.refs_0_, ...), custom_call_target="tpu_custom_call", output_to_operand_aliasing={{1}: (6, {}), {2}: (7, {}), {3}: (8, {}), {4}: (9, {})} | custom-call | tf_op jit(solution)/shard_map/combine/pallas_call | solution.py:575
Async XLA Ops:
  0.0 2.1 %collective-permute-start = (f32[128,128]{1,0:T(8,128)}, f32[128,128]{1,0:T(8,128)S(1)}, u32[]{:S(2)}, u32[]{:S(2)}) collective-permute-start(f32[128,128]{1,0:T(8,128)} %refs_0_.1), channel_id=1, source_target_pairs={{0,4},{4,0},{8,12},{12,8},{16,20},{20,16},{24,28},{28,24},{1,5},{5... | collective-permute-start | bytes 196616 | tf_op jit(solution)/shard_map/ppermute | solution.py:536

commit v10 on v9

--- a/solution.py
+++ b/solution.py
@@ -46,7 +46,7 @@
 SENT = 16
 LANES = 128
 OWN_ROWS, OTHER_ROWS, COL_ROWS = slice(0, 48), slice(48, 96), slice(96, 128)
-TILED_ROWS = [slice(128, 144)] * (LANES // SENT) + [slice(144, 160)] * (LANES // SENT)
+TILED_ROWS = slice(128, 256), slice(256, 384)
 PIECE = SENT // 2 + 1
 
 
@@ -307,8 +307,7 @@
     ]
     corners = dot3(
         split(jnp.concatenate([over_rows] + nears)),
-        [jnp.concatenate([table[i, rows] for rows in TILED_ROWS]) for i in range(2)],
-        NT,
+        [jnp.concatenate([table[i, rows] for rows in TILED_ROWS], axis=1) for i in range(2)],
     )
 
     def share(values):
@@ -473,10 +472,12 @@
             feature = products[row_stencil][:, width * col_stencil : width * (col_stencil + 1)]
             channel = len(FEATURES) * level + f
             staged[channel] = feature.astype(jnp.bfloat16)
-            copies.append(
-                pltpu.make_async_copy(staged.at[channel], out.at[channel], sems.at[channel])
-            )
-            copies[-1].start()
+            if f + 1 == len(FEATURES) or level:
+                done = pl.ds(channel, 1) if level else pl.ds(0, len(FEATURES))
+                copies.append(
+                    pltpu.make_async_copy(staged.at[done], out.at[done], sems.at[channel])
+                )
+                copies[-1].start()
     for copy in copies:
         copy.wait()
 
@@ -503,9 +504,11 @@
 
     gains = [[s**k for k in range(3)] for s in DEVIATIONS]
     single = summary_table(width)
-    sums = np.zeros((32 + 2 * SENT, width))
-    sums[:BASIS] = single
-    sums[32:] = np.concatenate([after(single), before(single)])
+    sums = np.zeros((32 + 2 * width, LANES))
+    sums[:BASIS, :width] = single
+    sums[32:] = np.concatenate(
+        [np.tile(part, (LANES // SENT, 1)).T for part in (after(single), before(single))]
+    )
     return operator_tables(width, cols, sources, gains), sums
 
 

time: 18.4 us -> 18.3 us (level)
  no operation moved by 1% of the time
where the time goes in v10:
time: 18.3 us; the launch traced here: 18.2 us
  blocking collectives  14.1 us (77%)
  Pallas kernels  3.64 us (20%)
  starting transfers between devices  0.45 us (2%)
    all_to_all x1, blocking collectives, on_device(): lax.all_to_all(sent.reshape(rows * cols, PIECE, 1, LANES), ('row', 'col')...  14.1 us
    pallas_call x1, Pallas kernels, on_device(): pl.pallas_call(lambda *refs: combine(rows, cols, *refs), out_shape=[jax.S...  1.67 us
    pallas_call x1, Pallas kernels, on_device(): pl.pallas_call(lambda *refs: prepare(rows, cols, *refs), out_shape=[pltpu...  1.66 us
    ppermute x1, starting transfers between devices, on_device(): other = lax.ppermute(image, 'row', [(i, i ^ 1) for i in range(rows)])  0.45 us
  transfers between devices with their start and end apart: 1, of which 0 were waited for; matrix products, arithmetic and copies ran while one was open for 0% of the time, Pallas kernels for 9%

profile of v10, /device:TPU:0, one launch (start us, length us, event | category | flops | bytes accessed | tf_op | source)
XLA Modules:
  0.0 18.2 jit_solution(7981715120529225579)
XLA Ops:
  0.0 0.5 %collective-permute-start = (f32[128,128]{1,0:T(8,128)}, f32[128,128]{1,0:T(8,128)S(1)}, u32[]{:S(2)}, u32[]{:S(2)}) collective-permute-start(f32[128,128]{1,0:T(8,128)} %refs_0_.1), channel_id=1, source_target_pairs={{0,4},{4,0},{8,12},{12,8},{16,20},{20,16},{24,28},{28,24},{1,5},{5... | collective-permute-start | bytes 196616 | tf_op jit(solution)/shard_map/ppermute | solution.py:539
  0.5 1.7 %prepare.1 = (f32[128,128]{1,0:T(8,128)S(1)}, bf16[2,384,128]{2,1,0:T(8,128)(2,1)S(1)}, bf16[2,3,128,384]{3,2,1,0:T(8,128)(2,1)S(1)}, bf16[2,128,768]{2,1,0:T(8,...) custom-call(f32[128,128]{1,0:T(8,128)} %refs_0_.1, ...), custom_call_target="tpu_custom_call" | custom-call | flops 7864320 | bytes 4194304 | tf_op jit(solution)/shard_map/prepare/pallas_call | solution.py:540
  2.1 0.0 collective-permute-done.refs_0_
  2.1 0.3 %pack.1 = (f32[288,128]{1,0:T(8,128)S(1)}, f32[16,128]{1,0:T(8,128)S(1)}) custom-call(f32[128,128]{1,0:T(8,128)S(1)} %collective-permute-done.refs_0_, bf16[2,384,128]{2,1,0:T(8,128)(2,1)S(1)} %get-tuple-element.17.refs_1_, f32[48,128]{1,0:T(8,128)S(1)} %get-tuple-element.18.refs_2_, f32[32,128]{1,0:T(8,128)S(1)} %get-tuple-element.19.refs_3_), custom_call_target="tpu_custom_call" | custom-call | tf_op jit(solution)/shard_map/pack/pallas_call | solution.py:558
  2.5 14.1 %all_to_all.5 = f32[32,9,1,128]{3,2,1,0:T(1,128)S(1)} all-to-all(f32[32,9,1,128]{3,2,1,0:T(1,128)S(1)} %bitcast.3), channel_id=1, replica_groups={{4,9,17,28,6,11,19,30,1,12,20,25,3,14,22,27,0,13,21,24,2,15,23,26,5,8,1..., dimensions={0} | all-to-all | bytes 294912 | tf_op jit(solution)/shard_map/all_to_all | solution.py:569
  16.5 1.7 %combine.1 = (bf16[12,128,128]{2,1,0:T(8,128)(2,1)}, bf16[2,3,128,384]{3,2,1,0:T(8,128)(2,1)S(1)}, bf16[2,128,768]{2,1,0:T(8,128)(2,1)S(1)}, bf16[2,64,768]{2,1,0:T(8,128)(2,1)S(1)}, f32[128,768]{1,0:T(8,128)S(1)}) custom-call(f32[128,128]{1,0:T(8,128)S(1)} %get-tuple-element.16.refs_0_, ...), custom_call_target="tpu_custom_call", output_to_operand_aliasing={{1}: (6, {}), {2}: (7, {}), {3}: (8, {}), {4}: (9, {})} | custom-call | tf_op jit(solution)/shard_map/combine/pallas_call | solution.py:578
Async XLA Ops:
  0.0 2.1 %collective-permute-start = (f32[128,128]{1,0:T(8,128)}, f32[128,128]{1,0:T(8,128)S(1)}, u32[]{:S(2)}, u32[]{:S(2)}) collective-permute-start(f32[128,128]{1,0:T(8,128)} %refs_0_.1), channel_id=1, source_target_pairs={{0,4},{4,0},{8,12},{12,8},{16,20},{20,16},{24,28},{28,24},{1,5},{5... | collective-permute-start | bytes 196616 | tf_op jit(solution)/shard_map/ppermute | solution.py:539
